TPU v7x, 32 devices: a whole 2x2x4 slice. The times are simulated.
32 devices in a mesh: req: 8 (over z, x), seq: 4 (over y, core).
Axes of the slice: x: 2, y: 2, z: 4, core: 2. Of those that a mesh axis runs over, the one named last changes fastest.
Arguments:
- x_in: bfloat16 [16384, 2560], P(('req', 'seq')), may hold values from -6 to 6
- bc_in: bfloat16 [16384, 256], P(('req', 'seq')), may hold values from -6 to 6
- z_in: bfloat16 [16384, 2560], P(('req', 'seq')), may hold values from -6 to 6
- dt_raw: bfloat16 [16384, 40], P(('req', 'seq')), may hold values from -3 to 22
- conv_weight: float32 [4, 2816], replicated, may hold values from -3 to 3
- conv_bias: float32 [2816], replicated, may hold values from -0.5 to 0.5
- dt_bias: float32 [40], replicated, may hold values from -5 to -4
- a_log: float32 [40], replicated, may hold values from -3.95 to 1.17
- d_skip: float32 [40], replicated, may hold values from 0.5 to 2
- norm_gain: float32 [2560], replicated, may hold values from 0.1 to 1.9
- w_out: bfloat16 [2560, 2560], replicated, may hold values from -0.125 to 0.125
- prompt_stretches: int32 [16], replicated, may hold values from 1 to 16, as said below
Outputs:
- mixed_out: bfloat16 [16384, 2560], P(('req', 'seq'))
- end_states: float32 [64, 40, 64, 128], P('req', 'seq')
Inputs may be any that keep to these rules, and one draw needn't show every extreme that they name: `prompt_stretches`: the lengths sum to 64; the last prompt is exactly 16 stretches long and none is longer.
All inputs are finite; a program needn't handle non-finite values.
Results may differ from a plain program's by a relative error of at most 0.0073.
Values may be sent and summed in bfloat16 or wider, within the bound.
A program may use at most 448 MiB of HBM per device.

v0:
```python
import jax
import jax.numpy as jnp
from jax import lax
from jax.sharding import PartitionSpec as P

N = 128
STRETCH = 256
LMAX_CH = 16


def from_behind(value, axis, steps):
    count = lax.axis_size(axis)
    leading, last = (max(0, -steps), min(count, count - steps))
    return lax.ppermute(value, axis, [(source, source + steps) for source in range(leading, last)])


def stretch_flags(prompt_stretches, stretch_ids):
    firsts = jnp.cumsum(prompt_stretches) - prompt_stretches
    last_stretches = firsts + prompt_stretches - 1
    starts = jnp.any(stretch_ids[:, None] == firsts[None, :], axis=1)
    finals = jnp.any(stretch_ids[:, None] == last_stretches[None, :], axis=1)
    return (starts, finals)


def causal_conv(row_block, history, weight, conv_bias, starts):
    conv_span = weight.shape[0]
    length = row_block.shape[0]
    extended = jnp.concatenate([history, row_block], axis=0)
    in_stretch = jnp.arange(length, dtype=jnp.int32) % STRETCH
    start_rows = jnp.repeat(starts, STRETCH)
    running = conv_bias[None, :]
    for offset in range(conv_span):
        lag_rows = conv_span - 1 - offset
        shifted = extended[offset : offset + length].astype(jnp.float32)
        usable = jnp.logical_not((in_stretch < lag_rows) & start_rows)
        running = running + weight[offset][None, :] * jnp.where(usable[:, None], shifted, 0.0)
    return jax.nn.silu(running).astype(jnp.bfloat16)


def local_stretch(x_stretch, bc_stretch, dt_stretch, dt_bias, a_log):
    state_size = bc_stretch.shape[1] // 2
    b_mat = bc_stretch[:, :state_size]
    c_mat = bc_stretch[:, state_size:]
    step_size = jax.nn.softplus(dt_stretch.astype(jnp.float32) + dt_bias[None, :])
    log_decay = jnp.cumsum(-jnp.exp(a_log)[None, :] * step_size, axis=0)
    scores = jnp.dot(c_mat, b_mat.T, preferred_element_type=jnp.float32)
    stretch_len = scores.shape[0]
    causal = jnp.arange(stretch_len)[:, None] >= jnp.arange(stretch_len)[None, :]
    by_head = log_decay.T
    segment = by_head[:, :, None] - by_head[:, None, :]
    decay_mask = jnp.where(causal[None], jnp.exp(jnp.where(causal[None], segment, 0.0)), 0.0)
    mixing = (scores[None] * decay_mask * step_size.T[:, None, :]).astype(jnp.bfloat16)
    y_diag = jnp.einsum("htu,uhp->thp", mixing, x_stretch, preferred_element_type=jnp.float32)
    tail_weight = jnp.exp(log_decay[-1][None, :] - log_decay) * step_size
    weighted_x = (x_stretch.astype(jnp.float32) * tail_weight[:, :, None]).astype(jnp.bfloat16)
    stretch_state = jnp.einsum("uhp,un->hpn", weighted_x, b_mat, preferred_element_type=jnp.float32)
    return (y_diag, stretch_state, log_decay)


def finish_stretch(y_diag, log_decay, state_in, x_stretch, c_mat, z_stretch, d_skip, norm_gain):
    state_low = state_in.astype(jnp.bfloat16)
    y_off = jnp.exp(log_decay)[:, :, None] * jnp.einsum(
        "tn,hpn->thp", c_mat, state_low, preferred_element_type=jnp.float32
    )
    mixed_rows = y_diag + y_off + d_skip[None, :, None] * x_stretch.astype(jnp.float32)
    mixed_rows = mixed_rows.reshape(mixed_rows.shape[0], -1)
    gated_rows = mixed_rows * jax.nn.silu(z_stretch.astype(jnp.float32))
    inv_rms = lax.rsqrt(jnp.mean(gated_rows * gated_rows, axis=-1, keepdims=True) + 1e-05)
    return (gated_rows * inv_rms * norm_gain[None, :]).astype(jnp.bfloat16)


def chain_states(earlier, later):
    return (earlier[0] * later[0], later[0][:, None, None] * earlier[1] + later[1])


def per_device(
    x_in,
    bc_in,
    z_in,
    dt_raw,
    conv_weight,
    conv_bias,
    dt_bias,
    a_log,
    d_skip,
    norm_gain,
    w_out,
    prompt_stretches,
):
    x_rows, bc_rows, z_rows, dt_rows = (
        lax.all_to_all(x_in, "req", split_axis=0, concat_axis=0, tiled=True),
        lax.all_to_all(bc_in, "req", split_axis=0, concat_axis=0, tiled=True),
        lax.all_to_all(z_in, "req", split_axis=0, concat_axis=0, tiled=True),
        lax.all_to_all(dt_raw, "req", split_axis=0, concat_axis=0, tiled=True),
    )
    row_count = x_rows.shape[0]
    inner_width = x_rows.shape[1]
    head_count = a_log.shape[0]
    head_dim = inner_width // head_count
    stretch_count = row_count // STRETCH
    conv_span = conv_weight.shape[0]
    device = lax.axis_index(("req", "seq"))
    stretch_ids = device * stretch_count + jnp.arange(stretch_count, dtype=jnp.int32)
    starts, finals = stretch_flags(prompt_stretches, stretch_ids)
    edge_x, edge_bc = from_behind(
        (x_rows[row_count - conv_span + 1 :], bc_rows[row_count - conv_span + 1 :]),
        ("req", "seq"),
        1,
    )
    conv_x = causal_conv(
        x_rows, edge_x, conv_weight[:, :inner_width], conv_bias[:inner_width], starts
    )
    conv_bc = causal_conv(
        bc_rows, edge_bc, conv_weight[:, inner_width:], conv_bias[inner_width:], starts
    )
    x_heads = conv_x.reshape(stretch_count, STRETCH, head_count, head_dim)
    bc_stretches = conv_bc.reshape(stretch_count, STRETCH, 2 * N)
    dt_stretches = dt_rows.reshape(stretch_count, STRETCH, head_count)

    def stretch_work(element):
        return local_stretch(element[0], element[1], element[2], dt_bias, a_log)

    y_diag, stretch_state, log_decay = lax.map(stretch_work, (x_heads, bc_stretches, dt_stretches))
    carried = jnp.where(starts[:, None], 0.0, jnp.exp(log_decay[:, -1, :]))
    total_gain = jnp.ones((head_count,), jnp.float32)
    total_state = jnp.zeros((head_count, head_dim, N), jnp.float32)
    for stretch in range(stretch_count):
        total_gain, total_state = chain_states(
            (total_gain, total_state), (carried[stretch], stretch_state[stretch])
        )
    device_total = lax.axis_size(("req", "seq"))
    reach = min(-(-(LMAX_CH - 1) // stretch_count), device_total - 1)
    incoming = from_behind((total_gain, total_state), ("req", "seq"), 1)
    covered = 1
    while covered < reach:
        farther = from_behind((incoming[0], incoming[1]), ("req", "seq"), covered)
        incoming = chain_states(farther, incoming)
        covered = covered * 2
    state_prev = incoming[1]
    normed_parts = []
    ending_parts = []
    for stretch in range(stretch_count):
        state_in = jnp.where(starts[stretch], jnp.zeros_like(state_prev), state_prev)
        z_stretch = z_rows[stretch * STRETCH : (stretch + 1) * STRETCH]
        normed_parts.append(
            finish_stretch(
                y_diag[stretch],
                log_decay[stretch],
                state_in,
                x_heads[stretch],
                bc_stretches[stretch, :, N:],
                z_stretch,
                d_skip,
                norm_gain,
            )
        )
        state_out = (
            jnp.exp(log_decay[stretch, -1])[:, None, None] * state_in + stretch_state[stretch]
        )
        ending_parts.append(jnp.where(finals[stretch], state_out, jnp.zeros_like(state_out)))
        state_prev = state_out
    normed = jnp.concatenate(normed_parts, axis=0)
    endings = lax.all_to_all(
        jnp.stack(ending_parts, axis=0), "seq", split_axis=1, concat_axis=0, tiled=True
    )
    projected = jnp.dot(normed, w_out, preferred_element_type=jnp.float32).astype(jnp.bfloat16)
    mixed_out = lax.all_to_all(projected, "req", split_axis=0, concat_axis=0, tiled=True)
    return (mixed_out, endings)


def solution(mesh):
    placed = (
        P(("req", "seq"), None),
        P(("req", "seq"), None),
        P(("req", "seq"), None),
        P(("req", "seq"), None),
        P(),
        P(),
        P(),
        P(),
        P(),
        P(),
        P(),
        P(),
    )
    return jax.shard_map(
        per_device,
        mesh=mesh,
        in_specs=placed,
        out_specs=(P(("req", "seq"), None), P("req", "seq", None, None)),
        check_vma=False,
    )
```

profile of v0, /device:TPU:0, one launch (start us, length us, event | category | flops | bytes accessed | tf_op | source)
XLA Modules:
  0.0 416.5 jit_solution(565917607180324382)
XLA Ops:
  1.7 13.8 %all_to_all.72 = bf16[8,2,1280]{2,1,0:T(2,128)(2,1)S(1)} all-to-all(bf16[8,2,1280]{2,1,0:T(2,128)(2,1)S(1)} %reshape.274), channel_id=1, replica_groups=mesh['req'=8,'seq'=4] {'req'}, dimensions={0} | all-to-all | bytes 81920 | tf_op jit(solution)/shard_map/all_to_all | solution.py:94
  15.5 11.5 %all_to_all.73 = bf16[8,64,256]{2,1,0:T(8,128)(2,1)S(1)} all-to-all(bf16[8,64,256]{2,1,0:T(8,128)(2,1)} %bitcast.239), channel_id=1, replica_groups=mesh['req'=8,'seq'=4] {'req'}, dimensions={0} | all-to-all | bytes 524288 | tf_op jit(solution)/shard_map/all_to_all | solution.py:92
  27.0 3.8 all-to-all-start
  33.2 55.0 %all-to-all-done = bf16[8,64,2560]{2,1,0:T(8,128)(2,1)S(1)} async-done(((bf16[8,64,2560]{2,1,0:T(8,128)(2,1)}), bf16[8,64,2560]{2,1,0:T(8,128)(2,1)S(1)}, u32[]{:S(2)}, u32[]{:S(2)}) %all-to-all-start) | async-done | bytes 2621472 | tf_op jit(solution)/shard_map/all_to_all | solution.py:91
  88.2 4.4 %all-to-all-start.3 = ((bf16[8,64,2560]{2,1,0:T(8,128)(2,1)}), bf16[8,64,2560]{2,1,0:T(8,128)(2,1)}, u32[]{:S(2)}, u32[]{:S(2)}) async-start(bf16[8,64,2560]{2,1,0:T(8,128)(2,1)} %bitcast.232), calls=%async_computation.3 | async-start | bytes 5242880 | tf_op jit(solution)/shard_map/all_to_all | solution.py:93
  92.6 1.3 collective-permute-start
  94.8 10.0 %multiply_convert_fusion.6 = bf16[512,2560]{1,0:T(8,128)(2,1)S(1)} fusion(bf16[512,2560]{1,0:T(8,128)(2,1)} %bitcast.224, bf16[3,2560]{1,0:T(4,128)(2,1)S(1)} %collective-permute-done, f32[2560]{0:T(1024)S(1)} %get-tuple-element.161, f32[2560]{0:T(1024)S(1)} %get-tuple-element.162, f32[2560]{0:T(1024)S(1)} %get-tuple-element.163, ...), kind=kLoop, calls=%fused_computation.45 | loop fusion | flops 39321600 | bytes 5311488 | tf_op jit(solution)/shard_map/convert_element_type | solution.py:37
  104.8 1.5 copy-done
  106.3 4.4 %reshape.263 = bf16[2,256,40,64]{3,2,1,0:T(8,128)(2,1)} reshape(bf16[512,2560]{1,0:T(8,128)(2,1)S(1)} %multiply_convert_fusion.6) | data formatting | bytes 5242880 | tf_op jit(solution)/shard_map/reshape | solution.py:116
  110.7 5.2 %copy.96 = bf16[2,256,40,64]{1,3,2,0:T(8,128)(2,1)S(1)} copy(bf16[2,256,40,64]{3,2,1,0:T(8,128)(2,1)} %reshape.263) | data formatting | bytes 5242880 | tf_op jit(solution)/shard_map/while | solution.py:123
  115.9 16.8 %while.16 = (s32[]{:T(128)}, f32[2,256,40,64]{1,3,2,0:T(8,128)}, f32[2,40,64,128]{3,2,1,0:T(8,128)}, f32[2,256,40]{1,2,0:T(8,128)S(1)}, bf16[2,256,40,64]{1,3,2,...) while((s32[]{:T(128)}, f32[2,256,40,64]{1,3,2,0:T(8,128)}, ...), condition=%wide.region_5.6_spmd, body=%wide.region_2.0_spmd.sunk | while | flops 539379840 | bytes 29302236 | solution.py:123
  117.5 4.7 %bitcast_dynamic-update-slice_fusion.4 = f32[2,256,40,64]{1,3,2,0:T(8,128)} fusion(f32[2,256,40,64]{1,3,2,0:T(8,128)} %get-tuple-element.297, s32[]{:T(128)} %get-tuple-element.296, f32[40,256]{1,0:T(8,128)S(1)} %get-tuple-element.282, f32[40,256]{1,0:T(8,128)S(1)} %get-tuple-element.283, f32[256,256]{1,0:T(8,128)S(1)} %fusion.97, ...), kind=kOutput, calls=%fused_computation.8.clone.1 | convolution fusion | flops 351272960 | bytes 4383744 | tf_op jit(solution)/shard_map/while/body/eval_jaxpr/htu,uhp->thp/dot_general | solution.py:53
  122.7 1.5 copy-done.6
  125.9 4.7 %bitcast_dynamic-update-slice_fusion.4 = f32[2,256,40,64]{1,3,2,0:T(8,128)} fusion(f32[2,256,40,64]{1,3,2,0:T(8,128)} %get-tuple-element.297, s32[]{:T(128)} %get-tuple-element.296, f32[40,256]{1,0:T(8,128)S(1)} %get-tuple-element.282, f32[40,256]{1,0:T(8,128)S(1)} %get-tuple-element.283, f32[256,256]{1,0:T(8,128)S(1)} %fusion.97, ...), kind=kOutput, calls=%fused_computation.8.clone.1 | convolution fusion | flops 351272960 | bytes 4383744 | tf_op jit(solution)/shard_map/while/body/eval_jaxpr/htu,uhp->thp/dot_general | solution.py:53
  131.1 1.5 copy-done.6
  133.0 1.9 bitcast_add_fusion.3
  134.9 4.2 %collective-permute-start.5 = (f32[40,64,128]{2,1,0:T(8,128)S(1)}, f32[40,64,128]{2,1,0:T(8,128)S(1)}, u32[]{:S(2)}, u32[]{:S(2)}) collective-permute-start(f32[40,64,128]{2,1,0:T(8,128)S(1)} %bitcast_add_fusion.3), channel_id=1, source_target_pairs={{0,1},{1,2},{2,3},{3,4},{4,5},{5,6},{6,7},{7,8},{8,9},{9,10},{10,1... | collective-permute-start | bytes 3932168 | tf_op jit(solution)/shard_map/ppermute | solution.py:14
  139.2 2.6 collective-permute-done.5
  141.8 16.2 %collective-permute-start.6 = (f32[40,64,128]{2,1,0:T(8,128)S(1)}, f32[40,64,128]{2,1,0:T(8,128)S(1)}, u32[]{:S(2)}, u32[]{:S(2)}) collective-permute-start(f32[40,64,128]{2,1,0:T(8,128)S(1)} %collective-permute-done.5), channel_id=1, source_target_pairs={{0,1},{1,2},{2,3},{3,4},{4,5},{5,6},{6,7},{7,8},{8,9},{9,10},{10,1... | collective-permute-start | bytes 3932168 | tf_op jit(solution)/shard_map/ppermute | solution.py:14
  157.9 4.6 %collective-permute-start.2 = (f32[40]{0:T(128)S(1)}, f32[40]{0:T(128)S(1)}, u32[]{:S(2)}, u32[]{:S(2)}) collective-permute-start(f32[40]{0:T(128)S(1)} %get-tuple-element.208), channel_id=1, source_target_pairs={{0,1},{1,2},{2,3},{3,4},{4,5},{5,6},{6,7},{7,8},{8,9},{9,10},{10,1... | collective-permute-start | bytes 488 | tf_op jit(solution)/shard_map/ppermute | solution.py:14
  163.6 20.5 %collective-permute-start.7 = (f32[40,64,128]{2,1,0:T(8,128)S(1)}, f32[40,64,128]{2,1,0:T(8,128)S(1)}, u32[]{:S(2)}, u32[]{:S(2)}) collective-permute-start(f32[40,64,128]{2,1,0:T(8,128)S(1)} %multiply_add_fusion.1), channel_id=1, source_target_pairs={{0,2},{1,3},{2,4},{3,5},{4,6},{5,7},{6,8},{7,9},{8,10},{9,11},{10,... | collective-permute-start | bytes 3932168 | tf_op jit(solution)/shard_map/ppermute | solution.py:14
  184.1 13.5 %collective-permute-start.3 = (f32[40]{0:T(128)S(1)}, f32[40]{0:T(128)S(1)}, u32[]{:S(2)}, u32[]{:S(2)}) collective-permute-start(f32[40]{0:T(128)S(1)} %collective-permute-done.2), channel_id=1, source_target_pairs={{0,1},{1,2},{2,3},{3,4},{4,5},{5,6},{6,7},{7,8},{8,9},{9,10},{10,1... | collective-permute-start | bytes 488 | tf_op jit(solution)/shard_map/ppermute | solution.py:14
  198.4 3.8 collective-permute-done.7
  203.5 31.0 %collective-permute-start.8 = (f32[40,64,128]{2,1,0:T(8,128)}, f32[40,64,128]{2,1,0:T(8,128)}, u32[]{:S(2)}, u32[]{:S(2)}) collective-permute-start(f32[40,64,128]{2,1,0:T(8,128)} %multiply_add_fusion), channel_id=1, source_target_pairs={{0,4},{1,5},{2,6},{3,7},{4,8},{5,9},{6,10},{7,11},{8,12},{9,13},{1... | collective-permute-start | bytes 3932168 | tf_op jit(solution)/shard_map/ppermute | solution.py:14
  234.5 3.9 slice_convert_fusion.2
  238.4 3.1 reshape.256
  241.5 6.0 %copy.101 = f32[256,40,64]{0,2,1:T(8,128)} copy(f32[256,40,64]{2,1,0:T(8,128)} %reshape.256) | data formatting | bytes 5242880 | tf_op jit(solution)/shard_map/convert_element_type | solution.py:67
  247.5 4.9 %reshape.259 = f32[256,40,64]{2,1,0:T(8,128)} reshape(f32[4,64,2560]{2,1,0:T(8,128)} %get-tuple-element.199) | data formatting | bytes 5242880 | tf_op jit(solution)/shard_map/convert_element_type | solution.py:67
  252.5 6.2 %copy.105 = f32[256,40,64]{0,2,1:T(8,128)} copy(f32[256,40,64]{2,1,0:T(8,128)} %reshape.259) | data formatting | bytes 5242880 | tf_op jit(solution)/shard_map/convert_element_type | solution.py:67
  258.9 3.0 slice_convert_fusion.3
  261.9 21.6 %collective-permute-start.4 = (f32[40]{0:T(128)S(1)}, f32[40]{0:T(128)S(1)}, u32[]{:S(2)}, u32[]{:S(2)}) collective-permute-start(f32[40]{0:T(128)S(1)} %mul.340), channel_id=1, source_target_pairs={{0,2},{1,3},{2,4},{3,5},{4,6},{5,7},{6,8},{7,9},{8,10},{9,11},{10,... | collective-permute-start | bytes 488 | tf_op jit(solution)/shard_map/ppermute | solution.py:14
  283.5 3.3 copy.98
  286.8 3.4 copy.102
  290.2 3.3 select_bitcast_fusion
  293.5 2.7 fusion.53
  296.2 1.5 fusion.51
  297.7 1.8 pad_maximum_fusion.1
  299.5 4.8 %all-to-all-start.5 = ((f32[2,40,64,128]{3,2,0,1:T(8,128)}), f32[2,40,64,128]{3,2,0,1:T(8,128)}, u32[]{:S(2)}, u32[]{:S(2)}) async-start(f32[2,40,64,128]{3,2,0,1:T(8,128)} %pad_maximum_fusion.1), calls=%async_computation.5 | async-start | bytes 5242880 | tf_op jit(solution)/shard_map/all_to_all | solution.py:163
  304.4 3.4 fusion.54
  307.8 7.2 %multiply_reduce_fusion.1 = (f32[256]{0:T(256)S(1)}, f32[256,40,64]{0,2,1:T(8,128)}, f32[256]{0:T(256)S(1)}, f32[256,40,64]{0,2,1:T(8,128)S(1)}) fusion(f32[256,40,64]{0,2,1:T(8,128)} %copy.101, f32[256,40,64]{0,2,1:T(8,128)S(1)} %bitcast.226, f32[40]{0:T(128)S(1)} %copy-done.15, f32[256,40,64]{0,2,1:T(8,128)S(1)} %fusion.54, ...), kind=kLoop, calls=%fused_computation.77 | loop fusion | flops 14417408 | bytes 26298528 | tf_op jit(solution)/shard_map/reduce_sum | solution.py:68
  315.0 2.1 copy.103
  317.1 3.4 copy.99
  320.5 4.3 %fusion.48 = (bf16[256,2560]{1,0:T(8,128)(2,1)S(1)}, bf16[256,2560]{1,0:T(8,128)(2,1)S(1)}) fusion(f32[256,2560]{1,0:T(8,128)} %copy.99, f32[4,64,2560]{2,1,0:T(8,128)S(1)} %copy-done.3, f32[2560]{0:T(1024)S(1)} %copy-done.13, f32[256]{0:T(256)S(1)} %add_rsqrt_fusion.1, f32[256]{0:T(256)S(1)} %add_rsqrt_fusion, f32[256,2560]{1,0:T(8,128)} %copy.103, ...), kind=kLoop, calls=%fused_computation.78 | loop fusion | flops 10485760 | bytes 13119488 | tf_op jit(solution)/shard_map/convert_element_type | solution.py:69
  324.9 11.0 %convolution_convert_fusion = bf16[512,2560]{1,0:T(8,128)(2,1)} fusion(bf16[2560,2560]{1,0:T(8,128)(2,1)} %param.24, bf16[256,2560]{1,0:T(8,128)(2,1)S(1)} %get-tuple-element.207, bf16[256,2560]{1,0:T(8,128)(2,1)S(1)} %get-tuple-element.206), kind=kOutput, calls=%fused_computation.46 | convolution fusion | flops 6717440000 | bytes 18350080 | tf_op jit(solution)/shard_map/dot_general | solution.py:166
  335.9 19.2 %all-to-all-start.4 = ((bf16[8,64,2560]{2,1,0:T(8,128)(2,1)}), bf16[8,64,2560]{2,1,0:T(8,128)(2,1)S(1)}, u32[]{:S(2)}, u32[]{:S(2)}) async-start(bf16[8,64,2560]{2,1,0:T(8,128)(2,1)} %bitcast.234), calls=%async_computation.4 | async-start | bytes 5242880 | tf_op jit(solution)/shard_map/all_to_all | solution.py:167
  355.1 3.6 copy.107
  358.7 56.3 %all-to-all-done.4 = bf16[8,64,2560]{2,1,0:T(8,128)(2,1)S(1)} async-done(((bf16[8,64,2560]{2,1,0:T(8,128)(2,1)}), bf16[8,64,2560]{2,1,0:T(8,128)(2,1)S(1)}, u32[]{:S(2)}, u32[]{:S(2)}) %all-to-all-start.4) | async-done | bytes 2621472 | tf_op jit(solution)/shard_map/all_to_all | solution.py:167
  415.0 1.5 copy.148
  (110 shorter events, 11.9 us)
Async XLA Ops:
  27.0 3.8 copy-start.14
  27.0 4.3 %copy-start.16 = (f32[40]{0:T(128)S(1)}, f32[40]{0:T(128)}, u32[]{:S(2)}) copy-start(f32[40]{0:T(128)} %param.21) | copy-start | bytes 484
  27.0 4.4 %copy-start.11 = (f32[4,2816]{1,0:T(4,128)S(1)}, f32[4,2816]{1,0:T(4,128)}, u32[]{:S(2)}) copy-start(f32[4,2816]{1,0:T(4,128)} %param.18) | copy-start | bytes 135172
  27.0 5.8 %copy-start.12 = (f32[2816]{0:T(1024)S(1)}, f32[2816]{0:T(1024)}, u32[]{:S(2)}) copy-start(f32[2816]{0:T(1024)} %param.19) | copy-start | bytes 33796
  27.0 61.1 %all-to-all-start = ((bf16[8,64,2560]{2,1,0:T(8,128)(2,1)}), bf16[8,64,2560]{2,1,0:T(8,128)(2,1)S(1)}, u32[]{:S(2)}, u32[]{:S(2)}) async-start(bf16[8,64,2560]{2,1,0:T(8,128)(2,1)} %bitcast.231), calls=%async_computation | async-start | bytes 5242880 | tf_op jit(solution)/shard_map/all_to_all | solution.py:91
  31.4 62.5 %collective-permute-start.1 = (bf16[3,256]{1,0:T(4,128)(2,1)S(1)}, bf16[3,256]{1,0:T(4,128)(2,1)S(1)}, u32[]{:S(2)}, u32[]{:S(2)}) collective-permute-start(bf16[3,256]{1,0:T(4,128)(2,1)S(1)} %slice.206), channel_id=1, source_target_pairs={{0,1},{1,2},{2,3},{3,4},{4,5},{5,6},{6,7},{7,8},{8,9},{9,10},{10,1... | collective-permute-start | bytes 4616 | tf_op jit(solution)/shard_map/ppermute | solution.py:14
  88.2 4.4 %copy-start.4 = (bf16[8,64,2560]{2,1,0:T(8,128)(2,1)}, bf16[8,64,2560]{2,1,0:T(8,128)(2,1)S(1)}, u32[]{:S(2)}) copy-start(bf16[8,64,2560]{2,1,0:T(8,128)(2,1)S(1)} %all-to-all-done) | copy-start | bytes 7864324
  88.2 146.4 %all-to-all-start.3 = ((bf16[8,64,2560]{2,1,0:T(8,128)(2,1)}), bf16[8,64,2560]{2,1,0:T(8,128)(2,1)}, u32[]{:S(2)}, u32[]{:S(2)}) async-start(bf16[8,64,2560]{2,1,0:T(8,128)(2,1)} %bitcast.232), calls=%async_computation.3 | async-start | bytes 5242880 | tf_op jit(solution)/shard_map/all_to_all | solution.py:93
  92.6 2.1 collective-permute-start
  104.8 1.5 copy-start
  110.7 5.2 %copy-start.10 = (f32[40]{0:T(128)S(1)}, f32[40]{0:T(128)}, u32[]{:S(2)}) copy-start(f32[40]{0:T(128)} %param.20) | copy-start | bytes 484
  117.5 4.7 %copy-start.5 = (f32[2,40,64,128]{3,2,1,0:T(8,128)S(1)}, f32[2,40,64,128]{3,2,1,0:T(8,128)}, u32[]{:S(2)}) copy-start(f32[2,40,64,128]{3,2,1,0:T(8,128)} %get-tuple-element.298) | copy-start | bytes 7864324 | tf_op jit(solution)/shard_map/while
  122.7 1.5 copy-start.6
  125.9 4.7 %copy-start.5 = (f32[2,40,64,128]{3,2,1,0:T(8,128)S(1)}, f32[2,40,64,128]{3,2,1,0:T(8,128)}, u32[]{:S(2)}) copy-start(f32[2,40,64,128]{3,2,1,0:T(8,128)} %get-tuple-element.298) | copy-start | bytes 7864324 | tf_op jit(solution)/shard_map/while
  131.1 1.5 copy-start.6
  134.9 6.8 %collective-permute-start.5 = (f32[40,64,128]{2,1,0:T(8,128)S(1)}, f32[40,64,128]{2,1,0:T(8,128)S(1)}, u32[]{:S(2)}, u32[]{:S(2)}) collective-permute-start(f32[40,64,128]{2,1,0:T(8,128)S(1)} %bitcast_add_fusion.3), channel_id=1, source_target_pairs={{0,1},{1,2},{2,3},{3,4},{4,5},{5,6},{6,7},{7,8},{8,9},{9,10},{10,1... | collective-permute-start | bytes 3932168 | tf_op jit(solution)/shard_map/ppermute | solution.py:14
  141.8 21.6 %collective-permute-start.6 = (f32[40,64,128]{2,1,0:T(8,128)S(1)}, f32[40,64,128]{2,1,0:T(8,128)S(1)}, u32[]{:S(2)}, u32[]{:S(2)}) collective-permute-start(f32[40,64,128]{2,1,0:T(8,128)S(1)} %collective-permute-done.5), channel_id=1, source_target_pairs={{0,1},{1,2},{2,3},{3,4},{4,5},{5,6},{6,7},{7,8},{8,9},{9,10},{10,1... | collective-permute-start | bytes 3932168 | tf_op jit(solution)/shard_map/ppermute | solution.py:14
  157.9 5.4 %collective-permute-start.2 = (f32[40]{0:T(128)S(1)}, f32[40]{0:T(128)S(1)}, u32[]{:S(2)}, u32[]{:S(2)}) collective-permute-start(f32[40]{0:T(128)S(1)} %get-tuple-element.208), channel_id=1, source_target_pairs={{0,1},{1,2},{2,3},{3,4},{4,5},{5,6},{6,7},{7,8},{8,9},{9,10},{10,1... | collective-permute-start | bytes 488 | tf_op jit(solution)/shard_map/ppermute | solution.py:14
  163.6 38.6 %collective-permute-start.7 = (f32[40,64,128]{2,1,0:T(8,128)S(1)}, f32[40,64,128]{2,1,0:T(8,128)S(1)}, u32[]{:S(2)}, u32[]{:S(2)}) collective-permute-start(f32[40,64,128]{2,1,0:T(8,128)S(1)} %multiply_add_fusion.1), channel_id=1, source_target_pairs={{0,2},{1,3},{2,4},{3,5},{4,6},{5,7},{6,8},{7,9},{8,10},{9,11},{10,... | collective-permute-start | bytes 3932168 | tf_op jit(solution)/shard_map/ppermute | solution.py:14
  184.1 14.3 %collective-permute-start.3 = (f32[40]{0:T(128)S(1)}, f32[40]{0:T(128)S(1)}, u32[]{:S(2)}, u32[]{:S(2)}) collective-permute-start(f32[40]{0:T(128)S(1)} %collective-permute-done.2), channel_id=1, source_target_pairs={{0,1},{1,2},{2,3},{3,4},{4,5},{5,6},{6,7},{7,8},{8,9},{9,10},{10,1... | collective-permute-start | bytes 488 | tf_op jit(solution)/shard_map/ppermute | solution.py:14
  203.5 86.7 %collective-permute-start.8 = (f32[40,64,128]{2,1,0:T(8,128)}, f32[40,64,128]{2,1,0:T(8,128)}, u32[]{:S(2)}, u32[]{:S(2)}) collective-permute-start(f32[40,64,128]{2,1,0:T(8,128)} %multiply_add_fusion), channel_id=1, source_target_pairs={{0,4},{1,5},{2,6},{3,7},{4,8},{5,9},{6,10},{7,11},{8,12},{9,13},{1... | collective-permute-start | bytes 3932168 | tf_op jit(solution)/shard_map/ppermute | solution.py:14
  238.4 3.1 copy-start.2
  252.5 6.4 %copy-start.1 = (bf16[512,2560]{1,0:T(8,128)(2,1)S(1)}, bf16[512,2560]{1,0:T(8,128)(2,1)}, u32[]{:S(2)}) copy-start(bf16[512,2560]{1,0:T(8,128)(2,1)} %copy-done) | copy-start | bytes 7864324
  261.9 28.2 %collective-permute-start.4 = (f32[40]{0:T(128)S(1)}, f32[40]{0:T(128)S(1)}, u32[]{:S(2)}, u32[]{:S(2)}) collective-permute-start(f32[40]{0:T(128)S(1)} %mul.340), channel_id=1, source_target_pairs={{0,2},{1,3},{2,4},{3,5},{4,6},{5,7},{6,8},{7,9},{8,10},{9,11},{10,... | collective-permute-start | bytes 488 | tf_op jit(solution)/shard_map/ppermute | solution.py:14
  286.8 3.4 copy-start.7
  299.5 36.4 %all-to-all-start.5 = ((f32[2,40,64,128]{3,2,0,1:T(8,128)}), f32[2,40,64,128]{3,2,0,1:T(8,128)}, u32[]{:S(2)}, u32[]{:S(2)}) async-start(f32[2,40,64,128]{3,2,0,1:T(8,128)} %pad_maximum_fusion.1), calls=%async_computation.5 | async-start | bytes 5242880 | tf_op jit(solution)/shard_map/all_to_all | solution.py:163
  304.3 3.5 copy-start.8
  304.3 3.5 copy-start.9
  304.4 3.5 copy-start.15
  317.1 3.4 copy-start.3
  317.1 3.4 copy-start.13
  335.9 79.1 %all-to-all-start.4 = ((bf16[8,64,2560]{2,1,0:T(8,128)(2,1)}), bf16[8,64,2560]{2,1,0:T(8,128)(2,1)S(1)}, u32[]{:S(2)}, u32[]{:S(2)}) async-start(bf16[8,64,2560]{2,1,0:T(8,128)(2,1)} %bitcast.234), calls=%async_computation.4 | async-start | bytes 5242880 | tf_op jit(solution)/shard_map/all_to_all | solution.py:167
where the time goes:
time: 418 us; the launch traced here: 416 us
  starting transfers between devices  147 us (35%)
  waiting for transfers between devices  119 us (28%)
  local copies, waits for them, and re-layouts  55.1 us (13%)
  other arithmetic  41.8 us (10%)
  matrix products  27.9 us (7%)
  blocking collectives  25.3 us (6%)
    ppermute x9, starting transfers between devices, from_behind(): lax.ppermute(value, axis, [(source, source + steps) for source in range(l...  114 us
    all_to_all x1, waiting for transfers between devices, per_device(): lax.all_to_all(projected, 'req', split_axis=0, concat_axis=0, tiled=True)  56.3 us
    all_to_all x1, waiting for transfers between devices, per_device(): lax.all_to_all(x_in, 'req', split_axis=0, concat_axis=0, tiled=True)  55 us
    convert_element_type x4, local copies, waits for them, and re-layouts, finish_stretch(): gated_rows = mixed_rows * jax.nn.silu(z_stretch.astype(jnp.float32))  20.3 us
    all_to_all x1, starting transfers between devices, per_device(): lax.all_to_all(projected, 'req', split_axis=0, concat_axis=0, tiled=True)  19.2 us
    all_to_all x1, blocking collectives, per_device(): lax.all_to_all(dt_raw, 'req', split_axis=0, concat_axis=0, tiled=True)  13.8 us
    all_to_all x1, blocking collectives, per_device(): lax.all_to_all(bc_in, 'req', split_axis=0, concat_axis=0, tiled=True)  11.5 us
    dot_general x1, matrix products, per_device(): jnp.dot(normed, w_out, preferred_element_type=jnp.float32)  11 us
  transfers between devices with their start and end apart: 13, of which 6 were waited for; matrix products, arithmetic and copies ran while one was open for 26% of the time, Pallas kernels for 0%

commit v1 on v0

v1 whole, which is shorter than its diff:
```python
import math

import jax
import jax.numpy as jnp
from jax import lax
from jax.experimental import pallas as pl
from jax.experimental.pallas import tpu as pltpu
from jax.sharding import PartitionSpec as P

N = 128
STRETCH = 256
LMAX_CH = 16
HEADS = 4
WIDTH = 256
HIST = 8
LOG2E = math.log2(math.e)


def conv_kernel(rows_ref, hist_ref, weight_ref, bias_ref, tail_ref, conv_ref, state_ref, b_mat):
    span = weight_ref.shape[0]
    extended = jnp.concatenate(
        [hist_ref[0].astype(jnp.float32), rows_ref[0].astype(jnp.float32)], axis=0
    )
    running = bias_ref[...]
    for offset in range(span):
        first = HIST - (span - 1) + offset
        running = running + weight_ref[offset : offset + 1, :] * extended[first : first + STRETCH]
    conv = (running * jax.nn.sigmoid(running)).astype(jnp.bfloat16)
    conv_ref[0] = conv

    @pl.when(pl.program_id(1) == 0)
    def _():
        b_mat[...] = conv[:, :N]

    @pl.when(pl.program_id(1) > 0)
    def _():
        lane = lax.broadcasted_iota(jnp.int32, (STRETCH, N), 1)
        for pair in range(HEADS // 2):
            tails = jnp.where(
                lane < N // 2,
                tail_ref[0, 0, :, 2 * pair : 2 * pair + 1],
                tail_ref[0, 0, :, 2 * pair + 1 : 2 * pair + 2],
            )
            weighted = (conv[:, pair * N : (pair + 1) * N].astype(jnp.float32) * tails).astype(
                jnp.bfloat16
            )
            state_ref[0, pair * N : (pair + 1) * N, :] = lax.dot_general(
                weighted, b_mat[...], (((0,), (0,)), ((), ())), preferred_element_type=jnp.float32
            ).astype(jnp.bfloat16)


def mix_kernel(x_ref, bc_ref, col_ref, row_ref, state_ref, skip_ref, y_ref, scores):
    half = STRETCH // 2

    @pl.when(pl.program_id(1) == 0)
    def _():
        scores[...] = lax.dot_general(
            bc_ref[0, :, N:], bc_ref[0, :, :N], (((1,), (1,)), ((), ())),
            preferred_element_type=jnp.float32,
        )

    lane = lax.broadcasted_iota(jnp.int32, (half, N), 1)
    low = lane < N // 2
    causal = lax.broadcasted_iota(jnp.int32, (half, half), 0) >= lax.broadcasted_iota(
        jnp.int32, (half, half), 1
    )
    c_mat = bc_ref[0, :, N:]
    for pair in range(HEADS // 2):
        lanes = slice(pair * N, (pair + 1) * N)
        x_pair = x_ref[0, :, lanes]
        y_off = lax.dot_general(
            c_mat, state_ref[0, lanes, :], (((1,), (1,)), ((), ())),
            preferred_element_type=jnp.float32,
        )
        tops, bottoms = [], []
        for head in (2 * pair, 2 * pair + 1):
            col = col_ref[0, 0, :, head : head + 1]
            row = row_ref[0, 0, head : head + 1, :]
            top = jnp.exp2(jnp.where(causal, col[:half] - row[:, :half], -1e30))
            top = (top * scores[:half, :half]).astype(jnp.bfloat16)
            tops.append(jnp.dot(top, x_pair[:half], preferred_element_type=jnp.float32))
            left = jnp.exp2(col[half:] - row[:, :half])
            left = (left * scores[half:, :half]).astype(jnp.bfloat16)
            right = jnp.exp2(jnp.where(causal, col[half:] - row[:, half:], -1e30))
            right = (right * scores[half:, half:]).astype(jnp.bfloat16)
            bottoms.append(
                jnp.dot(
                    jnp.concatenate([left, right], axis=1), x_pair,
                    preferred_element_type=jnp.float32,
                )
            )
        skip = skip_ref[:, lanes]
        for part, (first, second) in enumerate((tops, bottoms)):
            rows = slice(part * half, (part + 1) * half)
            decay = jnp.exp2(
                jnp.where(
                    low,
                    col_ref[0, 0, rows, 2 * pair : 2 * pair + 1],
                    col_ref[0, 0, rows, 2 * pair + 1 : 2 * pair + 2],
                )
            )
            y = jnp.where(low, first, second) + decay * y_off[rows]
            y = y + skip * x_pair[rows].astype(jnp.float32)
            y_ref[0, rows, lanes] = y.astype(jnp.bfloat16)


def conv_and_state(rows, history, weight, bias, tails, inner):
    blocks = inner // WIDTH
    channels = weight.shape[1]

    def column(block):
        return jnp.where(block == 0, blocks, block - 1)

    def earlier(block):
        return jnp.maximum(block - 1, 0)

    return pl.pallas_call(
        conv_kernel,
        grid=(2, blocks + 1),
        in_specs=[
            pl.BlockSpec((1, STRETCH, WIDTH), lambda i, b: (i, 0, column(b))),
            pl.BlockSpec((1, HIST, WIDTH), lambda i, b: (i, 0, column(b))),
            pl.BlockSpec((weight.shape[0], WIDTH), lambda i, b: (0, column(b))),
            pl.BlockSpec((1, WIDTH), lambda i, b: (0, column(b))),
            pl.BlockSpec((1, 1, STRETCH, HEADS), lambda i, b: (i, earlier(b), 0, 0)),
        ],
        out_specs=[
            pl.BlockSpec((1, STRETCH, WIDTH), lambda i, b: (i, 0, column(b))),
            pl.BlockSpec((1, WIDTH, N), lambda i, b: (i, earlier(b), 0)),
        ],
        out_shape=[
            jax.ShapeDtypeStruct((2, STRETCH, channels), jnp.bfloat16),
            jax.ShapeDtypeStruct((2, inner, N), jnp.bfloat16),
        ],
        scratch_shapes=[pltpu.VMEM((STRETCH, N), jnp.bfloat16)],
        name="conv_and_state",
    )(rows, history, weight, bias, tails)


def mix(conv, col, row, state_in, skip, inner):
    blocks = inner // WIDTH
    return pl.pallas_call(
        mix_kernel,
        grid=(2, blocks),
        in_specs=[
            pl.BlockSpec((1, STRETCH, WIDTH), lambda i, b: (i, 0, b)),
            pl.BlockSpec((1, STRETCH, WIDTH), lambda i, b: (i, 0, blocks)),
            pl.BlockSpec((1, 1, STRETCH, HEADS), lambda i, b: (i, b, 0, 0)),
            pl.BlockSpec((1, 1, HEADS, STRETCH), lambda i, b: (i, b, 0, 0)),
            pl.BlockSpec((1, WIDTH, N), lambda i, b: (i, b, 0)),
            pl.BlockSpec((1, WIDTH), lambda i, b: (0, b)),
        ],
        out_specs=pl.BlockSpec((1, STRETCH, WIDTH), lambda i, b: (i, 0, b)),
        out_shape=jax.ShapeDtypeStruct((2, STRETCH, inner), jnp.bfloat16),
        scratch_shapes=[pltpu.VMEM((STRETCH, STRETCH), jnp.float32)],
        name="mix",
    )(conv, conv, col, row, state_in, skip)


def per_device(
    x_in,
    bc_in,
    z_in,
    dt_raw,
    conv_weight,
    conv_bias,
    dt_bias,
    a_log,
    d_skip,
    norm_gain,
    w_out,
    prompt_stretches,
):
    n_req, n_seq = lax.axis_size("req"), lax.axis_size("seq")
    group = n_req // 2
    tokens, inner = x_in.shape
    heads = a_log.shape[0]
    head_dim = inner // heads
    span = conv_weight.shape[0]
    part = tokens // n_req
    req, seq = lax.axis_index("req"), lax.axis_index("seq")
    half, place = req // group, req % group
    same_half = [[h * group + q for q in range(group)] for h in range(2)]

    lengths = prompt_stretches
    firsts = jnp.cumsum(lengths) - lengths
    stretch_total = n_req * n_seq * 2
    every = jnp.arange(stretch_total, dtype=jnp.int32)
    all_starts = jnp.any(every[:, None] == firsts[None, :], axis=1)
    all_finals = jnp.any(every[:, None] == (firsts + lengths - 1)[None, :], axis=1)

    def gather_stretches(rows):
        cut = rows.reshape(2, group, part, rows.shape[-1])
        return lax.all_to_all(
            cut, "req", split_axis=1, concat_axis=1, tiled=True, axis_index_groups=same_half
        )

    packed = jnp.concatenate([x_in, bc_in, dt_raw], axis=1)
    rows = gather_stretches(packed).reshape(2, STRETCH, packed.shape[1])
    channels = inner + 2 * N

    def index_of(h, q, s):
        return (h * group + q) * n_seq + s

    moves = [[], []]
    for q in range(group):
        for s in range(n_seq):
            for slot in range(2):
                moves[slot].append((index_of(0, q, s), index_of(1, q, s)))
                if s + 1 < n_seq:
                    moves[slot].append((index_of(1, q, s), index_of(0, q, s + 1)))
        source = index_of(1, q, n_seq - 1)
        if q + 1 < group:
            for slot in range(2):
                moves[slot].append((source, index_of(0, q + 1, 0)))
        else:
            moves[0].append((source, index_of(0, 0, 0)))
    ends = rows[:, STRETCH - (span - 1) :, :channels]
    got = [lax.ppermute(ends[slot], ("req", "seq"), moves[slot]) for slot in range(2)]
    wrapped = (req == 0) & (seq == 0)
    own = (jnp.arange(2) * group + place) * (2 * n_seq) + 2 * seq + half
    history = jnp.stack(
        [jnp.where(wrapped, got[1], got[0]), jnp.where(wrapped, got[0], got[1])]
    )
    own_starts = all_starts[own]
    history = jnp.where(own_starts[:, None, None], jnp.zeros_like(history), history)
    history = jnp.pad(history, ((0, 0), (HIST - (span - 1), 0), (0, 0)))

    step = jax.nn.softplus(rows[:, :, channels:].astype(jnp.float32) + dt_bias)
    triangle = jnp.tril(jnp.ones((STRETCH, STRETCH), jnp.float32))
    log_decay = jnp.einsum(
        "tu,cuh->cth", triangle, -jnp.exp(a_log) * step, precision=lax.Precision.HIGHEST
    )
    last = log_decay[:, -1, :]
    tails = jnp.exp(last[:, None, :] - log_decay) * step

    def by_block(value):
        return value.reshape(2, STRETCH, heads // HEADS, HEADS)

    col = by_block(log_decay * LOG2E).transpose(0, 2, 1, 3)
    row = by_block(log_decay * LOG2E - jnp.log2(step)).transpose(0, 2, 3, 1)
    tails = by_block(tails).transpose(0, 2, 1, 3)

    gains = lax.all_gather(jnp.exp(last), ("req", "seq"), axis=0)
    gains = gains.reshape(2, group, n_seq, 2, heads).transpose(3, 1, 2, 0, 4)
    gains = gains.reshape(stretch_total, heads)
    heads_here = heads // n_seq
    gains = lax.dynamic_slice_in_dim(gains, seq * heads_here, heads_here, axis=1)
    gains = jnp.where(all_starts[:, None], 0.0, gains)

    conv, states = conv_and_state(rows, history, conv_weight, conv_bias[None, :], tails, inner)

    pairs = [
        [index_of(h, q, s) for h in range(2) for s in range(n_seq)] for q in range(group)
    ]

    def by_heads(value):
        value = value.reshape(2 * n_seq, heads_here * head_dim, N)
        return lax.all_to_all(
            value, ("req", "seq"), split_axis=0, concat_axis=0, tiled=True, axis_index_groups=pairs
        )

    held = by_heads(states).reshape(2, n_seq, heads_here, head_dim, N).astype(jnp.float32)
    held_count = 2 * n_seq
    first_held = req * held_count

    def gain_of(stretch):
        return gains[stretch][:, None, None]

    total = jnp.zeros((heads_here, head_dim, N), jnp.float32)
    for k in range(held_count):
        total = gain_of(first_held + k) * total + held[k % 2, k // 2]
    total = total.astype(jnp.bfloat16)
    reach = min(-(-(LMAX_CH - 1) // held_count), n_req - 1)
    incoming = jnp.zeros_like(total, jnp.float32)
    reach_gain = jnp.ones((heads_here,), jnp.float32)
    for steps in range(1, reach + 1):
        arrived = lax.ppermute(total, "req", [(i, i + steps) for i in range(n_req - steps)])
        incoming = incoming + reach_gain[:, None, None] * arrived.astype(jnp.float32)
        before = jnp.maximum(req - steps, 0) * held_count
        reach_gain = reach_gain * jnp.prod(
            lax.dynamic_slice_in_dim(gains, before, held_count, axis=0), axis=0
        )
    entering = [[None] * n_seq, [None] * n_seq]
    endings = []
    previous = incoming
    for k in range(held_count):
        start = all_starts[first_held + k]
        entering[k % 2][k // 2] = jnp.where(start, 0.0, previous).astype(jnp.bfloat16)
        previous = gain_of(first_held + k) * previous + held[k % 2, k // 2]
        endings.append(jnp.where(all_finals[first_held + k], previous, 0.0))
    endings = jnp.stack(endings)
    state_in = by_heads(jnp.stack(entering[0] + entering[1])).reshape(2, inner, N)

    skip = jnp.repeat(d_skip, head_dim)[None, :]
    y = mix(conv, col, row, state_in, skip, inner)
    y = gather_stretches(y.reshape(tokens, inner)).reshape(tokens, inner).astype(jnp.float32)
    gated = y * jax.nn.silu(z_in.astype(jnp.float32))
    inv_rms = lax.rsqrt(jnp.mean(gated * gated, axis=-1, keepdims=True) + 1e-05)
    normed = (gated * inv_rms * norm_gain[None, :]).astype(jnp.bfloat16)
    mixed_out = jnp.dot(normed, w_out, preferred_element_type=jnp.float32).astype(jnp.bfloat16)
    return (mixed_out, endings)


def solution(mesh):
    rows = P(("req", "seq"), None)
    return jax.shard_map(
        per_device,
        mesh=mesh,
        in_specs=(rows,) * 4 + (P(),) * 8,
        out_specs=(rows, P("req", "seq", None, None)),
        check_vma=False,
    )
```

time: 418 us -> 292 us (0.70)
  starting transfers between devices: 147 us -> 36.4 us
  Pallas kernels: 0 us -> 37.5 us
  local copies, waits for them, and re-layouts: 55.1 us -> 30 us
  blocking collectives: 25.3 us -> 49.9 us
  waiting for transfers between devices: 119 us -> 94.6 us
  matrix products: 27.9 us -> 11.8 us
  other arithmetic: 41.8 us -> 28.2 us
    ppermute x9 -> x4, starting transfers between devices: 114 us -> 17.1 us  [the longest x2 11.9 us: per_device(): lax.ppermute(total, 'req', [(i, i + steps) for i in range(n_req - steps)])]
    all_gather x0 -> x1, blocking collectives: none -> 49.9 us  [per_device(): gains = lax.all_gather(jnp.exp(last), ('req', 'seq'), axis=0)]
    pallas_call x0 -> x2, Pallas kernels: none -> 37.5 us  [the longest x1 20.5 us: conv_and_state(): pl.pallas_call(conv_kernel, grid=(2, blocks + 1), in_specs=[pl.BlockSpec(...]
    convert_element_type x6 -> x0, local copies, waits for them, and re-layouts: 26.9 us -> none  [the longest x4 20.3 us: finish_stretch(): gated_rows = mixed_rows * jax.nn.silu(z_stretch.astype(jnp.float32))]
    all_to_all x2 -> x0, blocking collectives: 25.3 us -> none  [the longest x1 13.8 us: per_device(): lax.all_to_all(dt_raw, 'req', split_axis=0, concat_axis=0, tiled=True)]
    all_to_all x4, waiting for transfers between devices: 111 us -> 90.8 us  [the longest x2 62.5 us: gather_stretches(): lax.all_to_all(cut, 'req', split_axis=1, concat_axis=1, tiled=True, axis_...]
    dot_general x8 -> x1, matrix products: 16.9 us -> 0.56 us  [per_device(): jnp.einsum('tu,cuh->cth', triangle, -jnp.exp(a_log) * step, precision=lax...]
    convert_element_type x5 -> x10, other arithmetic: 22 us -> 8.2 us  [the longest x8 5.38 us: per_device(): jnp.where(start, 0.0, previous).astype(jnp.bfloat16)]
  transfers between devices with their start and end apart: 13 -> 8, of which waited for: 6 -> 5; matrix products, arithmetic and copies ran while one was open for 26% -> 5% of each run, Pallas kernels for 0% -> 0%
where the time goes in v1:
time: 292 us; the launch traced here: 289 us
  waiting for transfers between devices  94.6 us (32%)
  blocking collectives  49.9 us (17%)
  Pallas kernels  37.5 us (13%)
  starting transfers between devices  36.4 us (12%)
  local copies, waits for them, and re-layouts  30 us (10%)
  other arithmetic  28.2 us (10%)
  matrix products  11.8 us (4%)
    all_to_all x2, waiting for transfers between devices, gather_stretches(): lax.all_to_all(cut, 'req', split_axis=1, concat_axis=1, tiled=True, axis_...  62.5 us
    all_gather x1, blocking collectives, per_device(): gains = lax.all_gather(jnp.exp(last), ('req', 'seq'), axis=0)  49.9 us
    all_to_all x2, waiting for transfers between devices, by_heads(): lax.all_to_all(value, ('req', 'seq'), split_axis=0, concat_axis=0, tiled=...  28.3 us
    pallas_call x1, Pallas kernels, conv_and_state(): pl.pallas_call(conv_kernel, grid=(2, blocks + 1), in_specs=[pl.BlockSpec(...  20.5 us
    pallas_call x1, Pallas kernels, mix(): pl.pallas_call(mix_kernel, grid=(2, blocks), in_specs=[pl.BlockSpec((1, S...  17 us
    ppermute x2, starting transfers between devices, per_device(): lax.ppermute(total, 'req', [(i, i + steps) for i in range(n_req - steps)])  11.9 us
    dot_general x1, matrix products, per_device(): jnp.dot(normed, w_out, preferred_element_type=jnp.float32)  11.3 us
    unnamed x7, other arithmetic  11 us
  transfers between devices with their start and end apart: 8, of which 5 were waited for; matrix products, arithmetic and copies ran while one was open for 5% of the time, Pallas kernels for 0%

profile of v1, /device:TPU:0, one launch (start us, length us, event | category | flops | bytes accessed | tf_op | source)
XLA Modules:
  0.0 289.4 jit_solution(8108856615718958269)
XLA Ops:
  0.6 0.9 copy.70
  1.5 2.0 pad_maximum_fusion
  3.6 1.9 copy.71
  5.5 5.4 %all-to-all-start = ((bf16[2,4,64,2856]{3,2,0,1:T(8,128)(2,1)}), bf16[2,4,64,2856]{3,2,0,1:T(8,128)(2,1)}, u32[]{:S(2)}, u32[]{:S(2)}) async-start(bf16[2,4,64,2856]{3,2,0,1:T(8,128)(2,1)} %copy.71), calls=%async_computation | async-start | bytes 6029312 | tf_op jit(solution)/shard_map/all_to_all | solution.py:194
  13.0 33.6 %all-to-all-done = bf16[2,4,64,2856]{3,2,0,1:T(8,128)(2,1)} async-done(((bf16[2,4,64,2856]{3,2,0,1:T(8,128)(2,1)}), bf16[2,4,64,2856]{3,2,0,1:T(8,128)(2,1)}, u32[]{:S(2)}, u32[]{:S(2)}) %all-to-all-start) | async-done | bytes 2924576 | tf_op jit(solution)/shard_map/all_to_all | solution.py:194
  46.6 2.1 copy.72
  48.7 0.7 slice_bitcast_fusion.9
  49.4 5.2 %collective-permute-start = (bf16[3,2816]{1,0:T(4,128)(2,1)}, bf16[3,2816]{1,0:T(4,128)(2,1)}, u32[]{:S(2)}, u32[]{:S(2)}) collective-permute-start(bf16[3,2816]{1,0:T(4,128)(2,1)} %get-tuple-element.26), channel_id=1, source_target_pairs={{0,16},{16,1},{1,17},{17,2},{2,18},{18,3},{3,19},{19,4},{4,20},{20... | collective-permute-start | bytes 50696 | tf_op jit(solution)/shard_map/ppermute | solution.py:219
  55.2 0.9 multiply_subtract_fusion
  56.2 1.7 copy.77
  57.8 3.2 %copy.78 = f32[2,256,10,4]{3,1,2,0:T(8,128)} copy(f32[2,256,10,4]{1,0,3,2:T(2,128)} %bitcast.188) | data formatting | bytes 163840 | tf_op jit(solution)/shard_map/reshape | solution.py:238
  61.0 0.8 collective-permute-done.1
  61.8 0.8 select_bitcast_fusion.1
  63.3 20.5 %conv_and_state.1 = (bf16[2,256,2816]{2,1,0:T(8,128)(2,1)}, bf16[2,2560,128]{2,1,0:T(8,128)(2,1)}) custom-call(bf16[2,256,2856]{2,1,0:T(8,128)(2,1)} %bitcast.171, bf16[2,8,2816]{2,1,0:T(8,128)(2,1)} %pad.4.hist_ref, f32[4,2816]{1,0:T(4,128)} %weight_ref.1, f32[1,2816]{1,0:T(1,128)} %broadcast_in_dim.73.bias_ref, f32[2,10,256,4]{3,2,1,0:T(8,128)} %bitcast.173), custom_call_target="tpu_custom_call" | custom-call | tf_op jit(solution)/shard_map/conv_and_state/pallas_call | solution.py:117
  83.8 4.4 %all-to-all-start.1 = ((bf16[8,640,128]{2,1,0:T(8,128)(2,1)}), bf16[8,640,128]{2,1,0:T(8,128)(2,1)S(1)}, u32[]{:S(2)}, u32[]{:S(2)}) async-start(bf16[8,640,128]{2,1,0:T(8,128)(2,1)} %bitcast.178), calls=%async_computation.1 | async-start | bytes 2621440 | tf_op jit(solution)/shard_map/all_to_all | solution.py:259
  88.2 49.9 %all-gather = f32[64,1,40]{2,1,0:T(1,128)S(1)} all-gather(f32[2,1,40]{2,1,0:T(1,128)S(1)} %get-tuple-element.28), channel_id=2, replica_groups=mesh['req'=8,'seq'=4] {'req','seq'}, dimensions={0}, use_global_device_ids=true | all-gather | bytes 10560 | tf_op jit(solution)/shard_map/all_gather | solution.py:244
  138.3 1.0 copy-done.3
  139.3 1.6 convert.2
  141.0 1.2 add_convert_fusion
  142.2 6.7 %collective-permute-start.2 = (bf16[10,64,128]{2,1,0:T(8,128)(2,1)}, bf16[10,64,128]{2,1,0:T(8,128)(2,1)S(1)}, u32[]{:S(2)}, u32[]{:S(2)}) collective-permute-start(bf16[10,64,128]{2,1,0:T(8,128)(2,1)} %add_convert_fusion), channel_id=1, source_target_pairs={{0,4},{4,8},{8,12},{12,16},{16,20},{20,24},{24,28},{1,5},{5,9},{9,... | collective-permute-start | bytes 491528 | tf_op jit(solution)/shard_map/ppermute | solution.py:278
  148.9 5.2 %collective-permute-start.3 = (bf16[10,64,128]{2,1,0:T(8,128)(2,1)}, bf16[10,64,128]{2,1,0:T(8,128)(2,1)S(1)}, u32[]{:S(2)}, u32[]{:S(2)}) collective-permute-start(bf16[10,64,128]{2,1,0:T(8,128)(2,1)} %add_convert_fusion), channel_id=1, source_target_pairs={{0,8},{4,12},{8,16},{12,20},{16,24},{20,28},{1,9},{5,13},{9,17},{1... | collective-permute-start | bytes 491528 | tf_op jit(solution)/shard_map/ppermute | solution.py:278
  154.2 0.7 fusion.27
  154.9 3.1 %collective-permute-done.3 = bf16[10,64,128]{2,1,0:T(8,128)(2,1)S(1)} collective-permute-done((bf16[10,64,128]{2,1,0:T(8,128)(2,1)}, bf16[10,64,128]{2,1,0:T(8,128)(2,1)S(1)}, u32[]{:S(2)}, u32[]{:S(2)}) %collective-permute-start.3) | collective-permute-done | bytes 163872 | tf_op jit(solution)/shard_map/ppermute | solution.py:278
  158.0 0.7 select_convert_fusion.7
  159.4 0.7 bitcast_dynamic-update-slice_fusion.7
  160.1 0.7 select_convert_fusion.3
  160.8 1.7 bitcast_dynamic-update-slice_fusion.6
  162.5 0.7 select_convert_fusion.6
  163.3 1.8 bitcast_dynamic-update-slice_fusion.5
  165.7 1.7 bitcast_dynamic-update-slice_fusion.4
  168.0 1.7 bitcast_dynamic-update-slice_fusion.3
  170.4 1.7 bitcast_dynamic-update-slice_fusion.2
  172.8 1.7 bitcast_dynamic-update-slice_fusion.1
  175.2 0.8 bitcast_dynamic-update-slice_fusion.14
  178.7 0.7 bitcast_dynamic-update-slice_fusion.9
  180.1 5.2 %all-to-all-start.2 = ((bf16[8,640,128]{2,1,0:T(8,128)(2,1)}), bf16[8,640,128]{2,1,0:T(8,128)(2,1)S(1)}, u32[]{:S(2)}, u32[]{:S(2)}) async-start(bf16[8,640,128]{2,1,0:T(8,128)(2,1)} %bitcast_dynamic-update-slice_fusion.8), calls=%async_computation.2 | async-start | bytes 2621440 | tf_op jit(solution)/shard_map/all_to_all | solution.py:259
  185.4 0.7 broadcast_in_dim_reshape.3.skip_ref
  186.2 2.3 copy.81
  189.2 28.3 %all-to-all-done.2 = bf16[8,640,128]{2,1,0:T(8,128)(2,1)S(1)} async-done(((bf16[8,640,128]{2,1,0:T(8,128)(2,1)}), bf16[8,640,128]{2,1,0:T(8,128)(2,1)S(1)}, u32[]{:S(2)}, u32[]{:S(2)}) %all-to-all-start.2) | async-done | bytes 1310752 | tf_op jit(solution)/shard_map/all_to_all | solution.py:259
  217.5 1.1 copy-done.2
  218.6 17.0 %mix.1 = bf16[2,256,2560]{2,1,0:T(8,128)(2,1)} custom-call(bf16[2,256,2816]{2,1,0:T(8,128)(2,1)} %get-tuple-element.4.x_ref.bc_ref, bf16[2,256,2816]{2,1,0:T(8,128)(2,1)} %get-tuple-element.4.x_ref.bc_ref, f32[2,10,256,4]{3,2,1,0:T(8,128)} %bitcast.174, f32[2,10,4,256]{3,2,1,0:T(4,128)} %bitcast.187, bf16[2,2560,128]{2,1,0:T(8,128)(2,1)} %bitcast.176, ...), custom_call_target="tpu_custom_call" | custom-call | tf_op jit(solution)/shard_map/mix/pallas_call | solution.py:142
  235.6 3.4 %copy.85 = bf16[2,4,64,2560]{3,2,0,1:T(8,128)(2,1)} copy(bf16[2,4,64,2560]{3,2,1,0:T(8,128)(2,1)} %bitcast.175) | data formatting | bytes 5242880 | tf_op jit(solution)/shard_map/reshape;reshape | solution.py:193
  239.0 4.3 %all-to-all-start.3 = ((bf16[2,4,64,2560]{3,2,0,1:T(8,128)(2,1)}), bf16[2,4,64,2560]{3,2,0,1:T(8,128)(2,1)S(1)}, u32[]{:S(2)}, u32[]{:S(2)}) async-start(bf16[2,4,64,2560]{3,2,0,1:T(8,128)(2,1)} %copy.85), calls=%async_computation.3 | async-start | bytes 5242880 | tf_op jit(solution)/shard_map/all_to_all | solution.py:194
  243.4 2.4 bitcast_dynamic-update-slice_fusion
  245.7 28.9 %all-to-all-done.3 = bf16[2,4,64,2560]{3,2,0,1:T(8,128)(2,1)S(1)} async-done(((bf16[2,4,64,2560]{3,2,0,1:T(8,128)(2,1)}), bf16[2,4,64,2560]{3,2,0,1:T(8,128)(2,1)S(1)}, u32[]{:S(2)}, u32[]{:S(2)}) %all-to-all-start.3) | async-done | bytes 2621472 | tf_op jit(solution)/shard_map/all_to_all | solution.py:194
  274.8 1.6 copy-done.4
  276.3 1.8 multiply_reduce_fusion
  278.2 11.3 %convolution_convert_fusion = bf16[512,2560]{1,0:T(8,128)(2,1)} fusion(bf16[2560,2560]{1,0:T(8,128)(2,1)} %param.22, f32[512,2560]{1,0:T(8,128)S(1)} %get-tuple-element.21, f32[2560]{0:T(1024)S(1)} %copy-done.11, f32[512]{0:T(512)S(1)} %add_rsqrt_fusion), kind=kOutput, calls=%fused_computation.9 | convolution fusion | flops 6716129280 | bytes 20983808 | tf_op jit(solution)/shard_map/dot_general | solution.py:301
  (64 shorter events, 12.2 us)
Async XLA Ops:
  5.5 5.4 %copy-start.7 = (s32[16]{0:T(128)S(1)}, s32[16]{0:T(128)}, u32[]{:S(2)}) copy-start(s32[16]{0:T(128)} %param.23) | copy-start | bytes 196
  5.5 5.6 %copy-start.6 = (f32[2816]{0:T(1024)S(1)}, f32[2816]{0:T(1024)}, u32[]{:S(2)}) copy-start(f32[2816]{0:T(1024)} %param.17) | copy-start | bytes 33796
  5.5 7.5 %copy-start.12 = (f32[40]{0:T(128)S(1)}, f32[40]{0:T(128)}, u32[]{:S(2)}) copy-start(f32[40]{0:T(128)} %param.19) | copy-start | bytes 484
  5.5 41.1 %all-to-all-start = ((bf16[2,4,64,2856]{3,2,0,1:T(8,128)(2,1)}), bf16[2,4,64,2856]{3,2,0,1:T(8,128)(2,1)}, u32[]{:S(2)}, u32[]{:S(2)}) async-start(bf16[2,4,64,2856]{3,2,0,1:T(8,128)(2,1)} %copy.71), calls=%async_computation | async-start | bytes 6029312 | tf_op jit(solution)/shard_map/all_to_all | solution.py:194
  13.0 41.6 %copy-start.8 = (f32[40]{0:T(128)S(1)}, f32[40]{0:T(128)}, u32[]{:S(2)}) copy-start(f32[40]{0:T(128)} %param.18) | copy-start | bytes 484
  48.7 12.3 %copy-start.1 = (bf16[2,4,64,2856]{3,2,1,0:T(8,128)(2,1)}, bf16[2,4,64,2856]{3,2,1,0:T(8,128)(2,1)S(1)}, u32[]{:S(2)}) copy-start(bf16[2,4,64,2856]{3,2,1,0:T(8,128)(2,1)S(1)} %copy.72) | copy-start | bytes 8773636
  49.4 11.6 %collective-permute-start = (bf16[3,2816]{1,0:T(4,128)(2,1)}, bf16[3,2816]{1,0:T(4,128)(2,1)}, u32[]{:S(2)}, u32[]{:S(2)}) collective-permute-start(bf16[3,2816]{1,0:T(4,128)(2,1)} %get-tuple-element.26), channel_id=1, source_target_pairs={{0,16},{16,1},{1,17},{17,2},{2,18},{18,3},{3,19},{19,4},{4,20},{20... | collective-permute-start | bytes 50696 | tf_op jit(solution)/shard_map/ppermute | solution.py:219
  54.6 7.1 %collective-permute-start.1 = (bf16[3,2816]{1,0:T(4,128)(2,1)}, bf16[3,2816]{1,0:T(4,128)(2,1)}, u32[]{:S(2)}, u32[]{:S(2)}) collective-permute-start(bf16[3,2816]{1,0:T(4,128)(2,1)} %get-tuple-element.27), channel_id=1, source_target_pairs={{0,16},{16,1},{1,17},{17,2},{2,18},{18,3},{3,19},{19,4},{4,20},{20... | collective-permute-start | bytes 50696 | tf_op jit(solution)/shard_map/ppermute | solution.py:219
  83.8 54.5 %all-to-all-start.1 = ((bf16[8,640,128]{2,1,0:T(8,128)(2,1)}), bf16[8,640,128]{2,1,0:T(8,128)(2,1)S(1)}, u32[]{:S(2)}, u32[]{:S(2)}) async-start(bf16[8,640,128]{2,1,0:T(8,128)(2,1)} %bitcast.178), calls=%async_computation.1 | async-start | bytes 2621440 | tf_op jit(solution)/shard_map/all_to_all | solution.py:259
  138.3 1.1 copy-start.3
  139.3 14.7 %copy-start.9 = (s32[16]{0:T(128)S(1)}, s32[16]{0:T(128)}, u32[]{:S(2)}) copy-start(s32[16]{0:T(128)} %get-tuple-element.56) | copy-start | bytes 196
  141.0 19.9 %copy-start = (f32[2,4,10,64,128]{4,3,2,1,0:T(8,128)}, f32[2,4,10,64,128]{4,3,2,1,0:T(8,128)S(1)}, u32[]{:S(2)}) copy-start(f32[2,4,10,64,128]{4,3,2,1,0:T(8,128)S(1)} %convert.2) | copy-start | bytes 7864324
  142.2 12.7 %collective-permute-start.2 = (bf16[10,64,128]{2,1,0:T(8,128)(2,1)}, bf16[10,64,128]{2,1,0:T(8,128)(2,1)S(1)}, u32[]{:S(2)}, u32[]{:S(2)}) collective-permute-start(bf16[10,64,128]{2,1,0:T(8,128)(2,1)} %add_convert_fusion), channel_id=1, source_target_pairs={{0,4},{4,8},{8,12},{12,16},{16,20},{20,24},{24,28},{1,5},{5,9},{9,... | collective-permute-start | bytes 491528 | tf_op jit(solution)/shard_map/ppermute | solution.py:278
  148.9 9.1 %collective-permute-start.3 = (bf16[10,64,128]{2,1,0:T(8,128)(2,1)}, bf16[10,64,128]{2,1,0:T(8,128)(2,1)S(1)}, u32[]{:S(2)}, u32[]{:S(2)}) collective-permute-start(bf16[10,64,128]{2,1,0:T(8,128)(2,1)} %add_convert_fusion), channel_id=1, source_target_pairs={{0,8},{4,12},{8,16},{12,20},{16,24},{20,28},{1,9},{5,13},{9,17},{1... | collective-permute-start | bytes 491528 | tf_op jit(solution)/shard_map/ppermute | solution.py:278
  174.5 4.9 %copy-start.5 = (f32[8,10,64,128]{3,2,1,0:T(8,128)}, f32[8,10,64,128]{3,2,1,0:T(8,128)S(1)}, u32[]{:S(2)}) copy-start(f32[8,10,64,128]{3,2,1,0:T(8,128)S(1)} %get-tuple-element.6) | copy-start | bytes 7864324
  174.5 10.8 %copy-start.10 = (f32[40]{0:T(128)S(1)}, f32[40]{0:T(128)}, u32[]{:S(2)}) copy-start(f32[40]{0:T(128)} %param.20) | copy-start | bytes 484
  180.1 37.4 %all-to-all-start.2 = ((bf16[8,640,128]{2,1,0:T(8,128)(2,1)}), bf16[8,640,128]{2,1,0:T(8,128)(2,1)S(1)}, u32[]{:S(2)}, u32[]{:S(2)}) async-start(bf16[8,640,128]{2,1,0:T(8,128)(2,1)} %bitcast_dynamic-update-slice_fusion.8), calls=%async_computation.2 | async-start | bytes 2621440 | tf_op jit(solution)/shard_map/all_to_all | solution.py:259
  217.5 1.1 copy-start.2
  239.0 35.6 %all-to-all-start.3 = ((bf16[2,4,64,2560]{3,2,0,1:T(8,128)(2,1)}), bf16[2,4,64,2560]{3,2,0,1:T(8,128)(2,1)S(1)}, u32[]{:S(2)}, u32[]{:S(2)}) async-start(bf16[2,4,64,2560]{3,2,0,1:T(8,128)(2,1)} %copy.85), calls=%async_computation.3 | async-start | bytes 5242880 | tf_op jit(solution)/shard_map/all_to_all | solution.py:194
  274.6 1.7 copy-start.4
  276.3 1.8 copy-start.11

commit v2 on v1

v2 whole, which is shorter than its diff:
```python
import math

import jax
import jax.numpy as jnp
from jax import lax
from jax.experimental import pallas as pl
from jax.experimental.pallas import tpu as pltpu
from jax.sharding import PartitionSpec as P

N = 128
STRETCH = 256
LMAX_CH = 16
HIST = 8
GAIN_ROWS = 16
VMEM = 40 * 1024 * 1024
LOG2E = math.log2(math.e)


def silu_conv(extended, weight_ref, bias_ref):
    span = weight_ref.shape[0]
    running = bias_ref[...]
    for offset in range(span):
        first = HIST - (span - 1) + offset
        running = running + weight_ref[offset : offset + 1, :] * extended[first : first + STRETCH]
    return (running * jax.nn.sigmoid(running)).astype(jnp.bfloat16)


def conv_kernel(
    rows_ref, hist_ref, weight_ref, bias_ref,
    bc_rows_ref, bc_hist_ref, bc_weight_ref, bc_bias_ref,
    tail_ref, gain_ref, conv_ref, bc_ref, state_ref,
):
    @pl.when(pl.program_id(1) == 0)
    def _():
        extended = jnp.concatenate(
            [bc_hist_ref[0].astype(jnp.float32), bc_rows_ref[0].astype(jnp.float32)], axis=0
        )
        bc_ref[0] = silu_conv(extended, bc_weight_ref, bc_bias_ref)

    extended = jnp.concatenate(
        [hist_ref[0].astype(jnp.float32), rows_ref[0].astype(jnp.float32)], axis=0
    )
    conv = silu_conv(extended, weight_ref, bias_ref)
    conv_ref[0] = conv
    b_mat = bc_ref[0, :, :N]
    lane = lax.broadcasted_iota(jnp.int32, (STRETCH, N), 1)
    width = conv.shape[1]
    for pair in range(width // N):
        tails = jnp.where(
            lane < N // 2,
            tail_ref[0, 0, :, 2 * pair : 2 * pair + 1],
            tail_ref[0, 0, :, 2 * pair + 1 : 2 * pair + 2],
        )
        weighted = (conv[:, pair * N : (pair + 1) * N].astype(jnp.float32) * tails).astype(
            jnp.bfloat16
        )
        state_ref[0, 0, pair * N : (pair + 1) * N, :] = lax.dot_general(
            weighted, b_mat, (((0,), (0,)), ((), ())), preferred_element_type=jnp.float32
        ).astype(jnp.bfloat16)
    state_ref[0, 0, width:, :] = gain_ref[0, 0]


def mix_kernel(x_ref, bc_ref, col_ref, row_ref, skip_ref, y_ref, scores):
    half = STRETCH // 2

    @pl.when(pl.program_id(1) == 0)
    def _():
        scores[...] = lax.dot_general(
            bc_ref[0, :, N:], bc_ref[0, :, :N], (((1,), (1,)), ((), ())),
            preferred_element_type=jnp.float32,
        )

    lane = lax.broadcasted_iota(jnp.int32, (half, N), 1)
    low = lane < N // 2
    causal = lax.broadcasted_iota(jnp.int32, (half, half), 0) >= lax.broadcasted_iota(
        jnp.int32, (half, half), 1
    )
    for pair in range(x_ref.shape[2] // N):
        lanes = slice(pair * N, (pair + 1) * N)
        x_pair = x_ref[0, :, lanes]
        tops, bottoms = [], []
        for head in (2 * pair, 2 * pair + 1):
            col = col_ref[0, 0, :, head : head + 1]
            row = row_ref[0, 0, head : head + 1, :]
            top = jnp.exp2(jnp.where(causal, col[:half] - row[:, :half], -1e30))
            top = (top * scores[:half, :half]).astype(jnp.bfloat16)
            tops.append(jnp.dot(top, x_pair[:half], preferred_element_type=jnp.float32))
            left = jnp.exp2(col[half:] - row[:, :half])
            left = (left * scores[half:, :half]).astype(jnp.bfloat16)
            right = jnp.exp2(jnp.where(causal, col[half:] - row[:, half:], -1e30))
            right = (right * scores[half:, half:]).astype(jnp.bfloat16)
            bottoms.append(
                jnp.dot(
                    jnp.concatenate([left, right], axis=1), x_pair,
                    preferred_element_type=jnp.float32,
                )
            )
        skip = skip_ref[:, lanes]
        for part, (first, second) in enumerate((tops, bottoms)):
            rows = slice(part * half, (part + 1) * half)
            y = jnp.where(low, first, second) + skip * x_pair[rows].astype(jnp.float32)
            y_ref[0, rows, lanes] = y


def carry_kernel(diag_ref, bc_ref, col_ref, state_ref, y_ref):
    c_mat = bc_ref[0, :, N:]
    low = lax.broadcasted_iota(jnp.int32, (STRETCH, N), 1) < N // 2
    for pair in range(diag_ref.shape[2] // N):
        lanes = slice(pair * N, (pair + 1) * N)
        y_off = lax.dot_general(
            c_mat, state_ref[0, 0, lanes, :], (((1,), (1,)), ((), ())),
            preferred_element_type=jnp.float32,
        )
        decay = jnp.exp2(
            jnp.where(
                low,
                col_ref[0, 0, :, 2 * pair : 2 * pair + 1],
                col_ref[0, 0, :, 2 * pair + 1 : 2 * pair + 2],
            )
        )
        y_ref[0, :, lanes] = (diag_ref[0, :, lanes] + decay * y_off).astype(jnp.bfloat16)


def gain_row(ref, index, rows):
    pieces = ref[index, rows : rows + GAIN_ROWS, :].astype(jnp.float32)
    return pieces[0:1] + pieces[1:2] + pieces[2:3]


def held_index(stretch, count):
    return (stretch % 2) * (count // 2) + stretch // 2


def total_kernel(starts_ref, held_ref, total_ref):
    count, rows = held_ref.shape[0], held_ref.shape[1] - GAIN_ROWS
    dim = N // 2
    gains = []
    for k in range(count):
        gain = gain_row(held_ref, held_index(k, count), rows)
        gains.append(jnp.where(starts_ref[k] > 0, 0.0, gain))
    product = gains[0]
    for k in range(1, count):
        product = product * gains[k]
    for head in range(rows // dim):
        span = slice(head * dim, (head + 1) * dim)
        total = held_ref[0, span, :].astype(jnp.float32)
        for k in range(1, count):
            total = gains[k][:, head : head + 1] * total + held_ref[
                held_index(k, count), span, :
            ].astype(jnp.float32)
        total_ref[span, :] = total.astype(jnp.bfloat16)
    high = product.astype(jnp.bfloat16).astype(jnp.float32)
    middle = (product - high).astype(jnp.bfloat16).astype(jnp.float32)
    rest = product - high - middle
    place = lax.broadcasted_iota(jnp.int32, (GAIN_ROWS, N), 0)
    total_ref[rows:, :] = jnp.where(
        place == 0, high, jnp.where(place == 1, middle, jnp.where(place == 2, rest, 0.0))
    ).astype(jnp.bfloat16)


def scan_kernel(starts_ref, finals_ref, held_ref, arrived_ref, state_ref, ending_ref):
    count, rows = held_ref.shape[0], held_ref.shape[1] - GAIN_ROWS
    dim = N // 2
    gains = [gain_row(held_ref, held_index(k, count), rows) for k in range(count)]
    reach = arrived_ref.shape[0]
    farther = [gain_row(arrived_ref, steps, rows) for steps in range(reach)]
    for head in range(rows // dim):
        span = slice(head * dim, (head + 1) * dim)
        state = arrived_ref[reach - 1, span, :].astype(jnp.float32)
        for steps in range(reach - 2, -1, -1):
            state = farther[steps][:, head : head + 1] * state + arrived_ref[
                steps, span, :
            ].astype(jnp.float32)
        for k in range(count):
            here = held_index(k, count)
            state = jnp.where(starts_ref[k] > 0, 0.0, state)
            state_ref[here, span, :] = state.astype(jnp.bfloat16)
            state = gains[k][:, head : head + 1] * state + held_ref[here, span, :].astype(
                jnp.float32
            )
            ending_ref[k, span, :] = jnp.where(finals_ref[k] > 0, state, 0.0)


def conv_and_state(rows, history, weight, bias, tails, gain_rows, inner):
    blocks = tails.shape[1]
    width = inner // blocks
    pair = 2 * N
    bc = inner // pair
    span = weight.shape[0]
    return pl.pallas_call(
        conv_kernel,
        grid=(2, blocks),
        in_specs=[
            pl.BlockSpec((1, STRETCH, width), lambda i, b: (i, 0, b)),
            pl.BlockSpec((1, HIST, width), lambda i, b: (i, 0, b)),
            pl.BlockSpec((span, width), lambda i, b: (0, b)),
            pl.BlockSpec((1, width), lambda i, b: (0, b)),
            pl.BlockSpec((1, STRETCH, pair), lambda i, b: (i, 0, bc)),
            pl.BlockSpec((1, HIST, pair), lambda i, b: (i, 0, bc)),
            pl.BlockSpec((span, pair), lambda i, b: (0, bc)),
            pl.BlockSpec((1, pair), lambda i, b: (0, bc)),
            pl.BlockSpec((1, 1) + tails.shape[2:], lambda i, b: (i, b, 0, 0)),
            pl.BlockSpec((1, 1, GAIN_ROWS, N), lambda i, b: (i, b, 0, 0)),
        ],
        out_specs=[
            pl.BlockSpec((1, STRETCH, width), lambda i, b: (i, 0, b)),
            pl.BlockSpec((1, STRETCH, pair), lambda i, b: (i, 0, 0)),
            pl.BlockSpec((1, 1, width + GAIN_ROWS, N), lambda i, b: (i, b, 0, 0)),
        ],
        out_shape=[
            jax.ShapeDtypeStruct((2, STRETCH, inner), jnp.bfloat16),
            jax.ShapeDtypeStruct((2, STRETCH, pair), jnp.bfloat16),
            jax.ShapeDtypeStruct((2, blocks, width + GAIN_ROWS, N), jnp.bfloat16),
        ],
        compiler_params=pltpu.CompilerParams(vmem_limit_bytes=VMEM),
        name="conv_and_state",
    )(rows, history, weight, bias, rows, history, weight, bias, tails, gain_rows)


def mix(conv, bc, col, row, skip):
    blocks = col.shape[1]
    width = conv.shape[2] // blocks
    return pl.pallas_call(
        mix_kernel,
        grid=(2, blocks),
        in_specs=[
            pl.BlockSpec((1, STRETCH, width), lambda i, b: (i, 0, b)),
            pl.BlockSpec((1, STRETCH, 2 * N), lambda i, b: (i, 0, 0)),
            pl.BlockSpec((1, 1) + col.shape[2:], lambda i, b: (i, b, 0, 0)),
            pl.BlockSpec((1, 1) + row.shape[2:], lambda i, b: (i, b, 0, 0)),
            pl.BlockSpec((1, width), lambda i, b: (0, b)),
        ],
        out_specs=pl.BlockSpec((1, STRETCH, width), lambda i, b: (i, 0, b)),
        out_shape=jax.ShapeDtypeStruct(conv.shape, jnp.float32),
        scratch_shapes=[pltpu.VMEM((STRETCH, STRETCH), jnp.float32)],
        compiler_params=pltpu.CompilerParams(vmem_limit_bytes=VMEM),
        cost_estimate=pl.CostEstimate(
            flops=15_000_000_000, bytes_accessed=8_000_000, transcendentals=5_000_000
        ),
        name="mix",
    )(conv, bc, col, row, skip)


def add_carried(diag, bc, col, state_in):
    blocks = col.shape[1]
    width = diag.shape[2] // blocks
    return pl.pallas_call(
        carry_kernel,
        grid=(2, blocks),
        in_specs=[
            pl.BlockSpec((1, STRETCH, width), lambda i, b: (i, 0, b)),
            pl.BlockSpec((1, STRETCH, 2 * N), lambda i, b: (i, 0, 0)),
            pl.BlockSpec((1, 1) + col.shape[2:], lambda i, b: (i, b, 0, 0)),
            pl.BlockSpec((1, 1, width, N), lambda i, b: (i, b, 0, 0)),
        ],
        out_specs=pl.BlockSpec((1, STRETCH, width), lambda i, b: (i, 0, b)),
        out_shape=jax.ShapeDtypeStruct(diag.shape, jnp.bfloat16),
        compiler_params=pltpu.CompilerParams(vmem_limit_bytes=VMEM),
        name="add_carried",
    )(diag, bc, col, state_in)


def held_total(starts, held):
    return pl.pallas_call(
        total_kernel,
        in_specs=[
            pl.BlockSpec(memory_space=pltpu.SMEM),
            pl.BlockSpec(memory_space=pltpu.VMEM),
        ],
        out_specs=pl.BlockSpec(memory_space=pltpu.VMEM),
        out_shape=jax.ShapeDtypeStruct(held.shape[1:], jnp.bfloat16),
        compiler_params=pltpu.CompilerParams(vmem_limit_bytes=VMEM),
        name="held_total",
    )(starts, held)


def held_scan(starts, finals, held, arrived):
    rows = held.shape[1] - GAIN_ROWS
    return pl.pallas_call(
        scan_kernel,
        in_specs=[pl.BlockSpec(memory_space=pltpu.SMEM)] * 2
        + [pl.BlockSpec(memory_space=pltpu.VMEM)] * 2,
        out_specs=[pl.BlockSpec(memory_space=pltpu.VMEM)] * 2,
        out_shape=[
            jax.ShapeDtypeStruct((held.shape[0], rows, N), jnp.bfloat16),
            jax.ShapeDtypeStruct((held.shape[0], rows, N), jnp.float32),
        ],
        compiler_params=pltpu.CompilerParams(vmem_limit_bytes=VMEM),
        name="held_scan",
    )(starts, finals, held, arrived)


def per_device(
    x_in,
    bc_in,
    z_in,
    dt_raw,
    conv_weight,
    conv_bias,
    dt_bias,
    a_log,
    d_skip,
    norm_gain,
    w_out,
    prompt_stretches,
):
    n_req, n_seq = lax.axis_size("req"), lax.axis_size("seq")
    group = n_req // 2
    tokens, inner = x_in.shape
    heads = a_log.shape[0]
    head_dim = inner // heads
    span = conv_weight.shape[0]
    part = tokens // n_req
    req, seq = lax.axis_index("req"), lax.axis_index("seq")
    half, place = req // group, req % group
    same_half = [[h * group + q for q in range(group)] for h in range(2)]

    lengths = prompt_stretches
    firsts = jnp.cumsum(lengths) - lengths
    stretch_total = n_req * n_seq * 2
    every = jnp.arange(stretch_total, dtype=jnp.int32)
    all_starts = jnp.any(every[:, None] == firsts[None, :], axis=1)
    all_finals = jnp.any(every[:, None] == (firsts + lengths - 1)[None, :], axis=1)

    def gather_stretches(rows):
        cut = rows.reshape(2, group, part, rows.shape[-1])
        return lax.all_to_all(
            cut, "req", split_axis=1, concat_axis=1, tiled=True, axis_index_groups=same_half
        )

    packed = jnp.concatenate([x_in, bc_in, dt_raw], axis=1)
    rows = gather_stretches(packed).reshape(2, STRETCH, packed.shape[1])
    channels = inner + 2 * N

    def index_of(h, q, s):
        return (h * group + q) * n_seq + s

    moves = []
    for q in range(group):
        for s in range(n_seq):
            moves.append((index_of(0, q, s), index_of(1, q, s)))
            following = index_of(0, q, s + 1) if s + 1 < n_seq else index_of(0, (q + 1) % group, 0)
            moves.append((index_of(1, q, s), following))
    got = lax.ppermute(rows[:, STRETCH - (span - 1) :, :channels], ("req", "seq"), moves)
    wrapped = (req == 0) & (seq == 0)
    history = jnp.where(wrapped, jnp.stack([jnp.zeros_like(got[0]), got[0]]), got)
    own = (jnp.arange(2) * group + place) * (2 * n_seq) + 2 * seq + half
    own_starts = all_starts[own]
    history = jnp.where(own_starts[:, None, None], jnp.zeros_like(history), history)
    history = jnp.pad(history, ((0, 0), (HIST - (span - 1), 0), (0, 0)))

    step = jax.nn.softplus(rows[:, :, channels:].astype(jnp.float32) + dt_bias)
    triangle = jnp.tril(jnp.ones((STRETCH, STRETCH), jnp.float32))
    log_decay = jnp.einsum(
        "tu,cuh->cth", triangle, -jnp.exp(a_log) * step, precision=lax.Precision.HIGHEST
    )
    last = log_decay[:, -1, :]
    tails = jnp.exp(last[:, None, :] - log_decay) * step

    heads_here = heads // n_seq

    def by_block(value):
        return value.reshape(2, STRETCH, n_seq, heads_here)

    col = by_block(log_decay * LOG2E).transpose(0, 2, 1, 3)
    row = by_block(log_decay * LOG2E - jnp.log2(step)).transpose(0, 2, 3, 1)
    tails = by_block(tails).transpose(0, 2, 1, 3)
    gain = jnp.exp(last).reshape(2, n_seq, 1, heads_here)
    high = lax.reduce_precision(gain, 8, 7)
    middle = lax.reduce_precision(gain - high, 8, 7)
    gain_rows = jnp.concatenate([high, middle, gain - high - middle], axis=2).astype(jnp.bfloat16)
    gain_rows = jnp.pad(gain_rows, ((0, 0), (0, 0), (0, GAIN_ROWS - 3), (0, N - heads_here)))

    conv, conv_bc, states = conv_and_state(
        rows, history, conv_weight, conv_bias[None, :], tails, gain_rows, inner
    )
    skip = jnp.repeat(d_skip, head_dim)[None, :]
    diag = mix(conv, conv_bc, col, row, skip)

    pairs = [
        [index_of(h, q, s) for h in range(2) for s in range(n_seq)] for q in range(group)
    ]

    def by_heads(value):
        return lax.all_to_all(
            value, ("req", "seq"), split_axis=0, concat_axis=0, tiled=True, axis_index_groups=pairs
        )

    held_count = 2 * n_seq
    held = by_heads(states.reshape(held_count, states.shape[2], N))
    held_starts = lax.dynamic_slice_in_dim(all_starts, req * held_count, held_count)
    held_finals = lax.dynamic_slice_in_dim(all_finals, req * held_count, held_count)
    held_starts = held_starts.astype(jnp.int32)
    total = held_total(held_starts, held)
    reach = min(-(-(LMAX_CH - 1) // held_count), n_req - 1)
    arrived = jnp.stack(
        [
            lax.ppermute(total, "req", [(i, i + steps) for i in range(n_req - steps)])
            for steps in range(1, reach + 1)
        ]
    )
    state_in, endings = held_scan(held_starts, held_finals.astype(jnp.int32), held, arrived)
    endings = endings.reshape(held_count, heads_here, head_dim, N)
    state_in = by_heads(state_in).reshape(2, n_seq, heads_here * head_dim, N)
    y = add_carried(diag, conv_bc, col, state_in)
    y = gather_stretches(y.reshape(tokens, inner)).reshape(tokens, inner).astype(jnp.float32)
    gated = y * jax.nn.silu(z_in.astype(jnp.float32))
    inv_rms = lax.rsqrt(jnp.mean(gated * gated, axis=-1, keepdims=True) + 1e-05)
    normed = (gated * inv_rms * norm_gain[None, :]).astype(jnp.bfloat16)
    mixed_out = jnp.dot(normed, w_out, preferred_element_type=jnp.float32).astype(jnp.bfloat16)
    return (mixed_out, endings)


def solution(mesh):
    rows = P(("req", "seq"), None)
    return jax.shard_map(
        per_device,
        mesh=mesh,
        in_specs=(rows,) * 4 + (P(),) * 8,
        out_specs=(rows, P("req", "seq", None, None)),
        check_vma=False,
    )
```

time: 292 us -> 211 us (0.72)
  other arithmetic: 28.2 us -> 5.59 us
  blocking collectives: 49.9 us -> 34 us
  starting transfers between devices: 36.4 us -> 22.2 us
  Pallas kernels: 37.5 us -> 25.1 us
  local copies, waits for them, and re-layouts: 30 us -> 20.6 us
    all_gather x1 -> x0, blocking collectives: 49.9 us -> none  [per_device(): gains = lax.all_gather(jnp.exp(last), ('req', 'seq'), axis=0)]
    all_to_all x0 -> x1, blocking collectives: none -> 34 us  [gather_stretches(): lax.all_to_all(cut, 'req', split_axis=1, concat_axis=1, tiled=True, axis_...]
    all_to_all x2 -> x1, waiting for transfers between devices: 62.5 us -> 34.7 us  [gather_stretches(): lax.all_to_all(cut, 'req', split_axis=1, concat_axis=1, tiled=True, axis_...]
    all_to_all x2, waiting for transfers between devices: 28.3 us -> 53.8 us  [by_heads(): lax.all_to_all(value, ('req', 'seq'), split_axis=0, concat_axis=0, tiled=...]
    unnamed x7 -> x1, other arithmetic: 11 us -> 0.01 us
    pallas_call x1, Pallas kernels: 17 us -> 6.24 us  [mix(): pl.pallas_call(mix_kernel, grid=(2, blocks), in_specs=[pl.BlockSpec((1, S...]
    convert_element_type x10 -> x2, other arithmetic: 8.2 us -> 0.15 us  [the longest x1 0.08 us: per_device(): held_starts = held_starts.astype(jnp.int32)]
    ppermute x2, starting transfers between devices: 11.9 us -> 3.89 us  [per_device(): lax.ppermute(total, 'req', [(i, i + steps) for i in range(n_req - steps)])]
  transfers between devices with their start and end apart: 8 -> 6, of which waited for: 5 -> 6; matrix products, arithmetic and copies ran while one was open for 5% -> 2% of each run, Pallas kernels for 0% -> 3%
where the time goes in v2:
time: 211 us
  waiting for transfers between devices  93.3 us (44%)
  blocking collectives  34 us (16%)
  Pallas kernels  25.1 us (12%)
  starting transfers between devices  22.2 us (11%)
  local copies, waits for them, and re-layouts  20.6 us (10%)
  matrix products  8.96 us (4%)
  other arithmetic  5.59 us (3%)
    all_to_all x2, waiting for transfers between devices, by_heads(): lax.all_to_all(value, ('req', 'seq'), split_axis=0, concat_axis=0, tiled=...  53.8 us
    all_to_all x1, waiting for transfers between devices, gather_stretches(): lax.all_to_all(cut, 'req', split_axis=1, concat_axis=1, tiled=True, axis_...  34.7 us
    all_to_all x1, blocking collectives, gather_stretches(): lax.all_to_all(cut, 'req', split_axis=1, concat_axis=1, tiled=True, axis_...  34 us
    unnamed x41, local copies, waits for them, and re-layouts  13.1 us
    pallas_call x1, Pallas kernels, conv_and_state(): pl.pallas_call(conv_kernel, grid=(2, blocks), in_specs=[pl.BlockSpec((1,...  10.6 us
    all_to_all x2, starting transfers between devices, by_heads(): lax.all_to_all(value, ('req', 'seq'), split_axis=0, concat_axis=0, tiled=...  10.1 us
    dot_general x1, matrix products, per_device(): jnp.dot(normed, w_out, preferred_element_type=jnp.float32)  8.41 us
    pallas_call x1, Pallas kernels, mix(): pl.pallas_call(mix_kernel, grid=(2, blocks), in_specs=[pl.BlockSpec((1, S...  6.24 us
  transfers between devices with their start and end apart: 6, of which 6 were waited for; matrix products, arithmetic and copies ran while one was open for 2% of the time, Pallas kernels for 3%

profile of v2, /device:TPU:0, one launch (start us, length us, event | category | flops | bytes accessed | tf_op | source)
XLA Modules:
  0.0 210.7 jit_solution(17301165229590991896)
XLA Ops:
  0.6 0.9 copy.79
  1.5 2.0 pad_maximum_fusion
  3.6 1.9 copy.80
  5.5 5.4 %all-to-all-start = ((bf16[2,4,64,2856]{3,2,0,1:T(8,128)(2,1)}), bf16[2,4,64,2856]{3,2,0,1:T(8,128)(2,1)}, u32[]{:S(2)}, u32[]{:S(2)}) async-start(bf16[2,4,64,2856]{3,2,0,1:T(8,128)(2,1)} %copy.80), calls=%async_computation | async-start | bytes 6029312 | tf_op jit(solution)/shard_map/all_to_all | solution.py:326
  10.8 0.1 copy.82
  11.0 0.1 reduce
  11.2 0.1 fusion.21
  11.3 0.6 gather_fusion
  11.9 34.7 %all-to-all-done = bf16[2,4,64,2856]{3,2,0,1:T(8,128)(2,1)} async-done(((bf16[2,4,64,2856]{3,2,0,1:T(8,128)(2,1)}), bf16[2,4,64,2856]{3,2,0,1:T(8,128)(2,1)}, u32[]{:S(2)}, u32[]{:S(2)}) %all-to-all-start) | async-done | bytes 2924576 | tf_op jit(solution)/shard_map/all_to_all | solution.py:326
  46.6 2.1 copy.81
  48.7 2.8 %collective-permute-start = (bf16[2,3,2816]{2,1,0:T(4,128)(2,1)S(1)}, bf16[2,3,2816]{2,1,0:T(4,128)(2,1)S(1)}, u32[]{:S(2)}, u32[]{:S(2)}) collective-permute-start(bf16[2,3,2816]{2,1,0:T(4,128)(2,1)S(1)} %slice.18), channel_id=1, source_target_pairs={{0,16},{16,1},{1,17},{17,2},{2,18},{18,3},{3,19},{19,4},{4,20},{20... | collective-permute-start | bytes 101384 | tf_op jit(solution)/shard_map/ppermute | solution.py:343
  51.5 0.6 convolution_bitcast_fusion
  52.1 1.0 multiply_subtract_fusion
  53.3 0.1 copy.86
  53.4 1.3 copy.87
  54.7 1.2 collective-permute-done
  56.0 0.1 select_select_fusion
  56.1 1.2 copy-done.2
  57.4 10.6 %conv_and_state.1 = (bf16[2,256,2560]{2,1,0:T(8,128)(2,1)S(1)}, bf16[2,256,256]{2,1,0:T(8,128)(2,1)S(1)}, bf16[2,4,656,128]{3,2,1,0:T(8,128)(2,1)S(1)}) custom-call(bf16[2,256,2856]{2,1,0:T(8,128)(2,1)S(1)} %bitcast.38, bf16[2,8,2816]{2,1,0:T(8,128)(2,1)S(1)} %pad.9.hist_ref.bc_hist_ref, f32[4,2816]{1,0:T(4,128)S(1)} %copy-done.4, ...), custom_call_target="tpu_custom_call" | custom-call | tf_op jit(solution)/shard_map/conv_and_state/pallas_call | solution.py:189
  68.0 1.1 copy-done.3
  69.1 1.5 copy-done.5
  70.5 3.6 %all-to-all-start.1 = ((bf16[8,656,128]{2,1,0:T(8,128)(2,1)}), bf16[8,656,128]{2,1,0:T(8,128)(2,1)S(1)}, u32[]{:S(2)}, u32[]{:S(2)}) async-start(bf16[8,656,128]{2,1,0:T(8,128)(2,1)} %bitcast.45), calls=%async_computation.1 | async-start | bytes 2686976 | tf_op jit(solution)/shard_map/all_to_all | solution.py:384
  74.2 32.8 %all-to-all-done.1.held_ref = bf16[8,656,128]{2,1,0:T(8,128)(2,1)S(1)} async-done(((bf16[8,656,128]{2,1,0:T(8,128)(2,1)}), bf16[8,656,128]{2,1,0:T(8,128)(2,1)S(1)}, u32[]{:S(2)}, u32[]{:S(2)}) %all-to-all-start.1) | async-done | bytes 1343520 | tf_op jit(solution)/shard_map/all_to_all | solution.py:384
  107.0 0.9 held_total.1
  107.8 1.3 collective-permute-start.2
  109.2 2.6 %collective-permute-start.1 = (bf16[656,128]{1,0:T(8,128)(2,1)S(1)}, bf16[656,128]{1,0:T(8,128)(2,1)S(1)}, u32[]{:S(2)}, u32[]{:S(2)}) collective-permute-start(bf16[656,128]{1,0:T(8,128)(2,1)S(1)} %held_total.1), channel_id=1, source_target_pairs={{0,4},{4,8},{8,12},{12,16},{16,20},{20,24},{24,28},{1,5},{5,9},{9,... | collective-permute-start | bytes 503816 | tf_op jit(solution)/shard_map/ppermute | solution.py:397
  111.8 0.1 fusion.22
  111.9 0.8 collective-permute-done.2
  112.8 2.7 %collective-permute-done.1 = bf16[656,128]{1,0:T(8,128)(2,1)S(1)} collective-permute-done((bf16[656,128]{1,0:T(8,128)(2,1)S(1)}, bf16[656,128]{1,0:T(8,128)(2,1)S(1)}, u32[]{:S(2)}, u32[]{:S(2)}) %collective-permute-start.1) | collective-permute-done | bytes 167968 | tf_op jit(solution)/shard_map/ppermute | solution.py:397
  115.6 3.1 %held_scan.1 = (bf16[8,640,128]{2,1,0:T(8,128)(2,1)}, f32[8,640,128]{2,1,0:T(8,128)}) custom-call(s32[8]{0:T(128)S(1)} %dynamic-slice_convert_fusion.1.starts_ref, s32[8]{0:T(128)S(1)} %dynamic-slice_convert_fusion.finals_ref, bf16[8,656,128]{2,1,0:T(8,128)(2,1)S(1)} %all-to-all-done.1.held_ref, bf16[2,656,128]{2,1,0:T(8,128)(2,1)S(1)} %pad_maximum_fusion.1.arrived_ref), custom_call_target="tpu_custom_call" | custom-call | tf_op jit(solution)/shard_map/held_scan/pallas_call | solution.py:278
  118.6 6.6 %all-to-all-start.2 = ((bf16[8,640,128]{2,1,0:T(8,128)(2,1)}), bf16[8,640,128]{2,1,0:T(8,128)(2,1)S(1)}, u32[]{:S(2)}, u32[]{:S(2)}) async-start(bf16[8,640,128]{2,1,0:T(8,128)(2,1)} %get-tuple-element.10), calls=%async_computation.2 | async-start | bytes 2621440 | tf_op jit(solution)/shard_map/all_to_all | solution.py:384
  125.3 0.1 broadcast_in_dim_reshape.3.skip_ref
  125.4 0.1 copy.93
  125.5 0.4 copy.94
  125.9 0.1 copy.96
  126.0 1.7 copy-done.6
  127.8 6.2 %mix.1.diag_ref = f32[2,256,2560]{2,1,0:T(8,128)S(1)} custom-call(bf16[2,256,2560]{2,1,0:T(8,128)(2,1)S(1)} %copy-done.6, bf16[2,256,256]{2,1,0:T(8,128)(2,1)S(1)} %get-tuple-element.8.bc_ref, f32[2,4,256,10]{3,2,1,0:T(8,128)S(1)} %bitcast.42, f32[2,4,10,256]{3,2,1,0:T(8,128)S(1)} %bitcast.46, f32[1,2560]{1,0:T(1,128)S(1)} %broadcast_in_dim_reshape.3.skip_ref), custom_call_target="tpu_custom_call" | custom-call | flops 15000000512 | bytes 8000000 | tf_op jit(solution)/shard_map/mix/pallas_call | solution.py:222
  134.0 2.3 %copy-done = f32[2,256,2560]{2,1,0:T(8,128)} copy-done((f32[2,256,2560]{2,1,0:T(8,128)}, f32[2,256,2560]{2,1,0:T(8,128)S(1)}, u32[]{:S(2)}) %copy-start) | copy-done | bytes 5242904
  136.3 21.1 %all-to-all-done.2 = bf16[8,640,128]{2,1,0:T(8,128)(2,1)S(1)} async-done(((bf16[8,640,128]{2,1,0:T(8,128)(2,1)}), bf16[8,640,128]{2,1,0:T(8,128)(2,1)S(1)}, u32[]{:S(2)}, u32[]{:S(2)}) %all-to-all-start.2) | async-done | bytes 1310752 | tf_op jit(solution)/shard_map/all_to_all | solution.py:384
  157.4 2.5 %copy-done.1 = f32[2,256,2560]{2,1,0:T(8,128)S(1)} copy-done((f32[2,256,2560]{2,1,0:T(8,128)S(1)}, f32[2,256,2560]{2,1,0:T(8,128)}, u32[]{:S(2)}) %copy-start.1) | copy-done | bytes 5242904
  159.9 4.3 %add_carried.1 = bf16[2,256,2560]{2,1,0:T(8,128)(2,1)S(1)} custom-call(f32[2,256,2560]{2,1,0:T(8,128)S(1)} %copy-done.1, bf16[2,256,256]{2,1,0:T(8,128)(2,1)S(1)} %get-tuple-element.8.bc_ref, f32[2,4,256,10]{3,2,1,0:T(8,128)S(1)} %bitcast.43, bf16[2,4,640,128]{3,2,1,0:T(8,128)(2,1)S(1)} %bitcast.41), custom_call_target="tpu_custom_call" | custom-call | tf_op jit(solution)/shard_map/add_carried/pallas_call | solution.py:246
  164.2 0.2 copy.98
  164.4 34.0 %all_to_all.20 = bf16[2,4,64,2560]{3,2,0,1:T(8,128)(2,1)S(1)} all-to-all(bf16[2,4,64,2560]{3,2,0,1:T(8,128)(2,1)S(1)} %copy.98), channel_id=1, replica_groups={{0,4,8,12},{16,20,24,28},{1,5,9,13},{17,21,25,29},{2,6,10,14},{18,22,26..., dimensions={1} | all-to-all | bytes 5242880 | tf_op jit(solution)/shard_map/all_to_all | solution.py:326
  198.4 0.3 copy.99
  198.6 1.5 copy-done.7
  200.1 1.8 multiply_reduce_fusion
  202.0 0.3 slice-done.3
  202.3 8.4 %convolution_convert_fusion = bf16[512,2560]{1,0:T(8,128)(2,1)} fusion(bf16[2560,2560]{1,0:T(8,128)(2,1)S(1)} %bitcast.59, f32[512,2560]{1,0:T(8,128)S(1)} %get-tuple-element.13, f32[2560]{0:T(1024)S(1)} %copy-done.14, f32[512]{0:T(512)S(1)} %add_rsqrt_fusion), kind=kOutput, calls=%fused_computation.9 | convolution fusion | flops 6716129280 | bytes 20983808 | tf_op jit(solution)/shard_map/dot_general | solution.py:409
  (54 shorter events, 0.7 us)
Async XLA Ops:
  5.5 5.4 %copy-start.11 = (s32[16]{0:T(128)S(1)}, s32[16]{0:T(128)}, u32[]{:S(2)}) copy-start(s32[16]{0:T(128)} %param.23) | copy-start | bytes 196
  5.5 5.6 %copy-start.10 = (f32[2816]{0:T(1024)S(1)}, f32[2816]{0:T(1024)}, u32[]{:S(2)}) copy-start(f32[2816]{0:T(1024)} %param.17) | copy-start | bytes 33796
  5.5 6.4 %copy-start.15 = (f32[40]{0:T(128)S(1)}, f32[40]{0:T(128)}, u32[]{:S(2)}) copy-start(f32[40]{0:T(128)} %param.19) | copy-start | bytes 484
  5.5 41.1 %all-to-all-start = ((bf16[2,4,64,2856]{3,2,0,1:T(8,128)(2,1)}), bf16[2,4,64,2856]{3,2,0,1:T(8,128)(2,1)}, u32[]{:S(2)}, u32[]{:S(2)}) async-start(bf16[2,4,64,2856]{3,2,0,1:T(8,128)(2,1)} %copy.80), calls=%async_computation | async-start | bytes 6029312 | tf_op jit(solution)/shard_map/all_to_all | solution.py:326
  11.9 39.6 %copy-start.12 = (f32[40]{0:T(128)S(1)}, f32[40]{0:T(128)}, u32[]{:S(2)}) copy-start(f32[40]{0:T(128)} %param.18) | copy-start | bytes 484
  48.7 7.4 %copy-start.4 = (f32[4,2816]{1,0:T(4,128)S(1)}, f32[4,2816]{1,0:T(4,128)}, u32[]{:S(2)}) copy-start(f32[4,2816]{1,0:T(4,128)} %bc_weight_ref.1) | copy-start | bytes 135172
  48.7 7.2 %collective-permute-start = (bf16[2,3,2816]{2,1,0:T(4,128)(2,1)S(1)}, bf16[2,3,2816]{2,1,0:T(4,128)(2,1)S(1)}, u32[]{:S(2)}, u32[]{:S(2)}) collective-permute-start(bf16[2,3,2816]{2,1,0:T(4,128)(2,1)S(1)} %slice.18), channel_id=1, source_target_pairs={{0,16},{16,1},{1,17},{17,2},{2,18},{18,3},{3,19},{19,4},{4,20},{20... | collective-permute-start | bytes 101384 | tf_op jit(solution)/shard_map/ppermute | solution.py:343
  56.1 1.2 copy-start.2
  68.0 1.1 copy-start.3
  69.1 1.5 copy-start.5
  70.5 36.4 %all-to-all-start.1 = ((bf16[8,656,128]{2,1,0:T(8,128)(2,1)}), bf16[8,656,128]{2,1,0:T(8,128)(2,1)S(1)}, u32[]{:S(2)}, u32[]{:S(2)}) async-start(bf16[8,656,128]{2,1,0:T(8,128)(2,1)} %bitcast.45), calls=%async_computation.1 | async-start | bytes 2686976 | tf_op jit(solution)/shard_map/all_to_all | solution.py:384
  74.2 51.0 %copy-start.13 = (f32[40]{0:T(128)S(1)}, f32[40]{0:T(128)}, u32[]{:S(2)}) copy-start(f32[40]{0:T(128)} %param.20) | copy-start | bytes 484
  74.2 51.2 %copy-start.9 = (f32[2,256,40]{2,1,0:T(8,128)S(1)}, f32[2,256,40]{2,1,0:T(8,128)}, u32[]{:S(2)}) copy-start(f32[2,256,40]{2,1,0:T(8,128)} %get-tuple-element.16) | copy-start | bytes 245764
  107.8 4.9 %collective-permute-start.2 = (bf16[656,128]{1,0:T(8,128)(2,1)S(1)}, bf16[656,128]{1,0:T(8,128)(2,1)S(1)}, u32[]{:S(2)}, u32[]{:S(2)}) collective-permute-start(bf16[656,128]{1,0:T(8,128)(2,1)S(1)} %held_total.1), channel_id=1, source_target_pairs={{0,8},{4,12},{8,16},{12,20},{16,24},{20,28},{1,9},{5,13},{9,17},{1... | collective-permute-start | bytes 503816 | tf_op jit(solution)/shard_map/ppermute | solution.py:397
  109.2 6.3 %collective-permute-start.1 = (bf16[656,128]{1,0:T(8,128)(2,1)S(1)}, bf16[656,128]{1,0:T(8,128)(2,1)S(1)}, u32[]{:S(2)}, u32[]{:S(2)}) collective-permute-start(bf16[656,128]{1,0:T(8,128)(2,1)S(1)} %held_total.1), channel_id=1, source_target_pairs={{0,4},{4,8},{8,12},{12,16},{16,20},{20,24},{24,28},{1,5},{5,9},{9,... | collective-permute-start | bytes 503816 | tf_op jit(solution)/shard_map/ppermute | solution.py:397
  115.5 10.3 %copy-start.8 = (f32[2,256,40]{2,1,0:T(8,128)S(1)}, f32[2,256,40]{2,1,0:T(8,128)}, u32[]{:S(2)}) copy-start(f32[2,256,40]{2,1,0:T(8,128)} %get-tuple-element.14) | copy-start | bytes 245764
  118.6 38.8 %all-to-all-start.2 = ((bf16[8,640,128]{2,1,0:T(8,128)(2,1)}), bf16[8,640,128]{2,1,0:T(8,128)(2,1)S(1)}, u32[]{:S(2)}, u32[]{:S(2)}) async-start(bf16[8,640,128]{2,1,0:T(8,128)(2,1)} %get-tuple-element.10), calls=%async_computation.2 | async-start | bytes 2621440 | tf_op jit(solution)/shard_map/all_to_all | solution.py:384
  126.0 1.7 copy-start.6
  134.0 2.3 %copy-start = (f32[2,256,2560]{2,1,0:T(8,128)}, f32[2,256,2560]{2,1,0:T(8,128)S(1)}, u32[]{:S(2)}) copy-start(f32[2,256,2560]{2,1,0:T(8,128)S(1)} %mix.1.diag_ref) | copy-start | bytes 15728644
  157.4 2.5 %copy-start.1 = (f32[2,256,2560]{2,1,0:T(8,128)S(1)}, f32[2,256,2560]{2,1,0:T(8,128)}, u32[]{:S(2)}) copy-start(f32[2,256,2560]{2,1,0:T(8,128)} %copy-done) | copy-start | bytes 15728644
  159.9 42.0 %slice-start = ((s8[13107200]{0:T(1024)(128)(4,1)}), s8[524288]{0:T(1024)(128)(4,1)S(1)}, s32[]{:S(2)}) async-start(s8[13107200]{0:T(1024)(128)(4,1)} %bitcast.58), calls=%async_computation.4 | async-start | bytes 1048576
  159.9 42.0 %slice-start.1 = ((s8[13107200]{0:T(1024)(128)(4,1)}), s8[4194304]{0:T(1024)(128)(4,1)S(1)}, s32[]{:S(2)}) async-start(s8[13107200]{0:T(1024)(128)(4,1)} %bitcast.58), calls=%async_computation.5 | async-start | bytes 8388608
  164.4 37.6 %slice-start.2 = ((s8[13107200]{0:T(1024)(128)(4,1)}), s8[4194304]{0:T(1024)(128)(4,1)S(1)}, s32[]{:S(2)}) async-start(s8[13107200]{0:T(1024)(128)(4,1)} %bitcast.58), calls=%async_computation.6 | async-start | bytes 8388608
  198.4 1.7 copy-start.7
  200.1 2.2 %slice-start.3 = ((s8[13107200]{0:T(1024)(128)(4,1)}), s8[4194304]{0:T(1024)(128)(4,1)S(1)}, s32[]{:S(2)}) async-start(s8[13107200]{0:T(1024)(128)(4,1)} %bitcast.58), calls=%async_computation.7 | async-start | bytes 8388608
  200.1 2.2 %copy-start.14 = (f32[2560]{0:T(1024)S(1)}, f32[2560]{0:T(1024)}, u32[]{:S(2)}) copy-start(f32[2560]{0:T(1024)} %param.21) | copy-start | bytes 30724

commit v3 on v2

--- a/solution.py
+++ b/solution.py
@@ -25,17 +25,19 @@
     return (running * jax.nn.sigmoid(running)).astype(jnp.bfloat16)
 
 
-def conv_kernel(
-    rows_ref, hist_ref, weight_ref, bias_ref,
-    bc_rows_ref, bc_hist_ref, bc_weight_ref, bc_bias_ref,
-    tail_ref, gain_ref, conv_ref, bc_ref, state_ref,
-):
-    @pl.when(pl.program_id(1) == 0)
-    def _():
-        extended = jnp.concatenate(
-            [bc_hist_ref[0].astype(jnp.float32), bc_rows_ref[0].astype(jnp.float32)], axis=0
-        )
-        bc_ref[0] = silu_conv(extended, bc_weight_ref, bc_bias_ref)
+def conv_kernel(*refs):
+    rows_ref, hist_ref, weight_ref, bias_ref, tail_ref, gain_ref = refs[:6]
+    if len(refs) == 9:
+        bc_ref, conv_ref, state_ref = refs[6:]
+    else:
+        bc_rows_ref, bc_hist_ref, bc_weight_ref, bc_bias_ref, conv_ref, state_ref, bc_ref = refs[6:]
+
+        @pl.when(pl.program_id(1) == 0)
+        def _():
+            extended = jnp.concatenate(
+                [bc_hist_ref[0].astype(jnp.float32), bc_rows_ref[0].astype(jnp.float32)], axis=0
+            )
+            bc_ref[0] = silu_conv(extended, bc_weight_ref, bc_bias_ref)
 
     extended = jnp.concatenate(
         [hist_ref[0].astype(jnp.float32), rows_ref[0].astype(jnp.float32)], axis=0
@@ -180,40 +182,56 @@
             ending_ref[k, span, :] = jnp.where(finals_ref[k] > 0, state, 0.0)
 
 
-def conv_and_state(rows, history, weight, bias, tails, gain_rows, inner):
+def conv_and_state(rows, history, weight, bias, tails, gain_rows, inner, conv_bc):
     blocks = tails.shape[1]
     width = inner // blocks
     pair = 2 * N
     bc = inner // pair
     span = weight.shape[0]
-    return pl.pallas_call(
-        conv_kernel,
-        grid=(2, blocks),
-        in_specs=[
-            pl.BlockSpec((1, STRETCH, width), lambda i, b: (i, 0, b)),
-            pl.BlockSpec((1, HIST, width), lambda i, b: (i, 0, b)),
-            pl.BlockSpec((span, width), lambda i, b: (0, b)),
-            pl.BlockSpec((1, width), lambda i, b: (0, b)),
+    in_specs = [
+        pl.BlockSpec((1, STRETCH, width), lambda i, b: (i, 0, b)),
+        pl.BlockSpec((1, HIST, width), lambda i, b: (i, 0, b)),
+        pl.BlockSpec((span, width), lambda i, b: (0, b)),
+        pl.BlockSpec((1, width), lambda i, b: (0, b)),
+        pl.BlockSpec((1, 1) + tails.shape[2:], lambda i, b: (i, b, 0, 0)),
+        pl.BlockSpec((1, 1, GAIN_ROWS, N), lambda i, b: (i, b, 0, 0)),
+    ]
+    out_specs = [
+        pl.BlockSpec((1, STRETCH, width), lambda i, b: (i, 0, b)),
+        pl.BlockSpec((1, 1, width + GAIN_ROWS, N), lambda i, b: (i, b, 0, 0)),
+    ]
+    out_shape = [
+        jax.ShapeDtypeStruct((2, STRETCH, inner), jnp.bfloat16),
+        jax.ShapeDtypeStruct((2, blocks, width + GAIN_ROWS, N), jnp.bfloat16),
+    ]
+    args = [rows, history, weight, bias, tails, gain_rows]
+    bc_spec = pl.BlockSpec((1, STRETCH, pair), lambda i, b: (i, 0, 0))
+    if conv_bc is None:
+        in_specs += [
             pl.BlockSpec((1, STRETCH, pair), lambda i, b: (i, 0, bc)),
             pl.BlockSpec((1, HIST, pair), lambda i, b: (i, 0, bc)),
             pl.BlockSpec((span, pair), lambda i, b: (0, bc)),
             pl.BlockSpec((1, pair), lambda i, b: (0, bc)),
-            pl.BlockSpec((1, 1) + tails.shape[2:], lambda i, b: (i, b, 0, 0)),
-            pl.BlockSpec((1, 1, GAIN_ROWS, N), lambda i, b: (i, b, 0, 0)),
-        ],
-        out_specs=[
-            pl.BlockSpec((1, STRETCH, width), lambda i, b: (i, 0, b)),
-            pl.BlockSpec((1, STRETCH, pair), lambda i, b: (i, 0, 0)),
-            pl.BlockSpec((1, 1, width + GAIN_ROWS, N), lambda i, b: (i, b, 0, 0)),
-        ],
-        out_shape=[
-            jax.ShapeDtypeStruct((2, STRETCH, inner), jnp.bfloat16),
-            jax.ShapeDtypeStruct((2, STRETCH, pair), jnp.bfloat16),
-            jax.ShapeDtypeStruct((2, blocks, width + GAIN_ROWS, N), jnp.bfloat16),
-        ],
+        ]
+        args += [rows, history, weight, bias]
+        out_specs.append(bc_spec)
+        out_shape.append(jax.ShapeDtypeStruct((2, STRETCH, pair), jnp.bfloat16))
+    else:
+        in_specs.append(bc_spec)
+        args.append(conv_bc)
+    made = pl.pallas_call(
+        conv_kernel,
+        grid=(2, blocks),
+        in_specs=in_specs,
+        out_specs=out_specs,
+        out_shape=out_shape,
         compiler_params=pltpu.CompilerParams(vmem_limit_bytes=VMEM),
+        cost_estimate=pl.CostEstimate(
+            flops=6_000_000_000, bytes_accessed=5_000_000, transcendentals=1_000_000
+        ),
         name="conv_and_state",
-    )(rows, history, weight, bias, rows, history, weight, bias, tails, gain_rows)
+    )(*args)
+    return made if conv_bc is None else (*made, conv_bc)
 
 
 def mix(conv, bc, col, row, skip):
@@ -234,7 +252,7 @@
         scratch_shapes=[pltpu.VMEM((STRETCH, STRETCH), jnp.float32)],
         compiler_params=pltpu.CompilerParams(vmem_limit_bytes=VMEM),
         cost_estimate=pl.CostEstimate(
-            flops=15_000_000_000, bytes_accessed=8_000_000, transcendentals=5_000_000
+            flops=4_000_000_000, bytes_accessed=4_000_000, transcendentals=2_000_000
         ),
         name="mix",
     )(conv, bc, col, row, skip)
@@ -327,9 +345,24 @@
             cut, "req", split_axis=1, concat_axis=1, tiled=True, axis_index_groups=same_half
         )
 
-    packed = jnp.concatenate([x_in, bc_in, dt_raw], axis=1)
+    heads_here = heads // n_seq
+    chunk = inner // n_seq
+    cut = 2 * (heads_here // 4 + 1)
+    parts = [(0, cut), (cut, heads_here)]
+
+    def columns(value, first, end, base=0):
+        return [
+            value[..., base + s * chunk + first * head_dim : base + s * chunk + end * head_dim]
+            for s in range(n_seq)
+        ]
+
+    packed = jnp.concatenate(columns(x_in, *parts[0]) + [bc_in, dt_raw], axis=1)
     rows = gather_stretches(packed).reshape(2, STRETCH, packed.shape[1])
-    channels = inner + 2 * N
+    second = jnp.concatenate(columns(x_in, *parts[1]), axis=1)
+    second, _ = lax.optimization_barrier((second, rows))
+    second_rows = gather_stretches(second).reshape(2, STRETCH, second.shape[1])
+    width = cut * head_dim * n_seq
+    channels = width + 2 * N
 
     def index_of(h, q, s):
         return (h * group + q) * n_seq + s
@@ -340,13 +373,20 @@
             moves.append((index_of(0, q, s), index_of(1, q, s)))
             following = index_of(0, q, s + 1) if s + 1 < n_seq else index_of(0, (q + 1) % group, 0)
             moves.append((index_of(1, q, s), following))
-    got = lax.ppermute(rows[:, STRETCH - (span - 1) :, :channels], ("req", "seq"), moves)
-    wrapped = (req == 0) & (seq == 0)
-    history = jnp.where(wrapped, jnp.stack([jnp.zeros_like(got[0]), got[0]]), got)
     own = (jnp.arange(2) * group + place) * (2 * n_seq) + 2 * seq + half
     own_starts = all_starts[own]
-    history = jnp.where(own_starts[:, None, None], jnp.zeros_like(history), history)
-    history = jnp.pad(history, ((0, 0), (HIST - (span - 1), 0), (0, 0)))
+    wrapped = (req == 0) & (seq == 0)
+
+    def history_of(ends):
+        got = lax.ppermute(ends, ("req", "seq"), moves)
+        history = jnp.where(wrapped, jnp.stack([jnp.zeros_like(got[0]), got[0]]), got)
+        history = jnp.where(own_starts[:, None, None], jnp.zeros_like(history), history)
+        return jnp.pad(history, ((0, 0), (HIST - (span - 1), 0), (0, 0)))
+
+    histories = [
+        history_of(rows[:, STRETCH - (span - 1) :, :channels]),
+        history_of(second_rows[:, STRETCH - (span - 1) :, :]),
+    ]
 
     step = jax.nn.softplus(rows[:, :, channels:].astype(jnp.float32) + dt_bias)
     triangle = jnp.tril(jnp.ones((STRETCH, STRETCH), jnp.float32))
@@ -356,8 +396,6 @@
     last = log_decay[:, -1, :]
     tails = jnp.exp(last[:, None, :] - log_decay) * step
 
-    heads_here = heads // n_seq
-
     def by_block(value):
         return value.reshape(2, STRETCH, n_seq, heads_here)
 
@@ -368,13 +406,7 @@
     high = lax.reduce_precision(gain, 8, 7)
     middle = lax.reduce_precision(gain - high, 8, 7)
     gain_rows = jnp.concatenate([high, middle, gain - high - middle], axis=2).astype(jnp.bfloat16)
-    gain_rows = jnp.pad(gain_rows, ((0, 0), (0, 0), (0, GAIN_ROWS - 3), (0, N - heads_here)))
-
-    conv, conv_bc, states = conv_and_state(
-        rows, history, conv_weight, conv_bias[None, :], tails, gain_rows, inner
-    )
     skip = jnp.repeat(d_skip, head_dim)[None, :]
-    diag = mix(conv, conv_bc, col, row, skip)
 
     pairs = [
         [index_of(h, q, s) for h in range(2) for s in range(n_seq)] for q in range(group)
@@ -386,23 +418,50 @@
         )
 
     held_count = 2 * n_seq
-    held = by_heads(states.reshape(held_count, states.shape[2], N))
     held_starts = lax.dynamic_slice_in_dim(all_starts, req * held_count, held_count)
     held_finals = lax.dynamic_slice_in_dim(all_finals, req * held_count, held_count)
     held_starts = held_starts.astype(jnp.int32)
-    total = held_total(held_starts, held)
+    held_finals = held_finals.astype(jnp.int32)
     reach = min(-(-(LMAX_CH - 1) // held_count), n_req - 1)
-    arrived = jnp.stack(
-        [
-            lax.ppermute(total, "req", [(i, i + steps) for i in range(n_req - steps)])
-            for steps in range(1, reach + 1)
-        ]
-    )
-    state_in, endings = held_scan(held_starts, held_finals.astype(jnp.int32), held, arrived)
-    endings = endings.reshape(held_count, heads_here, head_dim, N)
-    state_in = by_heads(state_in).reshape(2, n_seq, heads_here * head_dim, N)
-    y = add_carried(diag, conv_bc, col, state_in)
-    y = gather_stretches(y.reshape(tokens, inner)).reshape(tokens, inner).astype(jnp.float32)
+    conv_bc = None
+    y_parts, ending_parts = [], []
+    for index, (first, end) in enumerate(parts):
+        count = end - first
+        inner_part = count * head_dim * n_seq
+        tail_columns = [conv_weight[:, inner:]] if index == 0 else []
+        weight = jnp.concatenate(columns(conv_weight, first, end) + tail_columns, axis=1)
+        tail_columns = [conv_bias[inner:]] if index == 0 else []
+        bias = jnp.concatenate(columns(conv_bias, first, end) + tail_columns)[None, :]
+        gain_part = jnp.pad(
+            gain_rows[..., first:end], ((0, 0), (0, 0), (0, GAIN_ROWS - 3), (0, N - count))
+        )
+        conv, states, conv_bc = conv_and_state(
+            (rows, second_rows)[index], histories[index], weight, bias,
+            tails[..., first:end], gain_part, inner_part, conv_bc,
+        )
+        col_part = col[..., first:end]
+        skip_part = jnp.concatenate(columns(skip, first, end), axis=1)
+        diag = mix(conv, conv_bc, col_part, row[:, :, first:end, :], skip_part)
+        held = by_heads(states.reshape(held_count, states.shape[2], N))
+        total = held_total(held_starts, held)
+        arrived = jnp.stack(
+            [
+                lax.ppermute(total, "req", [(i, i + steps) for i in range(n_req - steps)])
+                for steps in range(1, reach + 1)
+            ]
+        )
+        state_in, endings = held_scan(held_starts, held_finals, held, arrived)
+        ending_parts.append(endings.reshape(held_count, count, head_dim, N))
+        state_in = by_heads(state_in).reshape(2, n_seq, count * head_dim, N)
+        y = add_carried(diag, conv_bc, col_part, state_in)
+        y_parts.append(gather_stretches(y.reshape(tokens, inner_part)).reshape(tokens, inner_part))
+    endings = jnp.concatenate(ending_parts, axis=1)
+    pieces = []
+    for s in range(n_seq):
+        for (first, end), y in zip(parts, y_parts):
+            size = (end - first) * head_dim
+            pieces.append(y[:, s * size : (s + 1) * size])
+    y = jnp.concatenate(pieces, axis=1).astype(jnp.float32)
     gated = y * jax.nn.silu(z_in.astype(jnp.float32))
     inv_rms = lax.rsqrt(jnp.mean(gated * gated, axis=-1, keepdims=True) + 1e-05)
     normed = (gated * inv_rms * norm_gain[None, :]).astype(jnp.bfloat16)

time: 211 us -> 231 us (1.095)
  starting transfers between devices: 22.2 us -> 51.5 us
  waiting for transfers between devices: 93.3 us -> 76 us
  blocking collectives: 34 us -> 19.5 us
  local copies, waits for them, and re-layouts: 20.6 us -> 32.4 us
  matrix products: 8.96 us -> 14.3 us
  Pallas kernels: 25.1 us -> 29.2 us
    all_to_all x2 -> x3, waiting for transfers between devices: 53.8 us -> 14.1 us  [by_heads(): lax.all_to_all(value, ('req', 'seq'), split_axis=0, concat_axis=0, tiled=...]
    all_to_all x1, blocking collectives: 34 us -> 19.5 us  [by_heads(): lax.all_to_all(value, ('req', 'seq'), split_axis=0, concat_axis=0, tiled=...]
    all_to_all x1 -> x4, starting transfers between devices: 5.35 us -> 18.4 us  [gather_stretches(): lax.all_to_all(cut, 'req', split_axis=1, concat_axis=1, tiled=True, axis_...]
    all_to_all x2 -> x3, starting transfers between devices: 10.1 us -> 21.3 us  [by_heads(): lax.all_to_all(value, ('req', 'seq'), split_axis=0, concat_axis=0, tiled=...]
    ppermute x1 -> x2, waiting for transfers between devices: 1.22 us -> 9.32 us  [history_of(): got = lax.ppermute(ends, ('req', 'seq'), moves)]
    all_to_all x1 -> x4, waiting for transfers between devices: 34.7 us -> 42 us  [gather_stretches(): lax.all_to_all(cut, 'req', split_axis=1, concat_axis=1, tiled=True, axis_...]
    ppermute x2 -> x4, waiting for transfers between devices: 3.58 us -> 10.6 us  [per_device(): lax.ppermute(total, 'req', [(i, i + steps) for i in range(n_req - steps)])]
    dot_general x1, matrix products: 8.41 us -> 13.8 us  [per_device(): jnp.dot(normed, w_out, preferred_element_type=jnp.float32)]
  transfers between devices with their start and end apart: 6 -> 13, of which waited for: 6 -> 9; matrix products, arithmetic and copies ran while one was open for 2% -> 6% of each run, Pallas kernels for 3% -> 11%
where the time goes in v3:
time: 231 us; the launch traced here: 230 us
  waiting for transfers between devices  76 us (33%)
  starting transfers between devices  51.5 us (22%)
  local copies, waits for them, and re-layouts  32.4 us (14%)
  Pallas kernels  29.2 us (13%)
  blocking collectives  19.5 us (8%)
  matrix products  14.3 us (6%)
  other arithmetic  5.4 us (2%)
    all_to_all x4, waiting for transfers between devices, gather_stretches(): lax.all_to_all(cut, 'req', split_axis=1, concat_axis=1, tiled=True, axis_...  42 us
    all_to_all x3, starting transfers between devices, by_heads(): lax.all_to_all(value, ('req', 'seq'), split_axis=0, concat_axis=0, tiled=...  21.3 us
    all_to_all x1, blocking collectives, by_heads(): lax.all_to_all(value, ('req', 'seq'), split_axis=0, concat_axis=0, tiled=...  19.5 us
    all_to_all x4, starting transfers between devices, gather_stretches(): lax.all_to_all(cut, 'req', split_axis=1, concat_axis=1, tiled=True, axis_...  18.4 us
    unnamed x67, local copies, waits for them, and re-layouts  14.5 us
    all_to_all x3, waiting for transfers between devices, by_heads(): lax.all_to_all(value, ('req', 'seq'), split_axis=0, concat_axis=0, tiled=...  14.1 us
    dot_general x1, matrix products, per_device(): jnp.dot(normed, w_out, preferred_element_type=jnp.float32)  13.8 us
    pallas_call x2, Pallas kernels, conv_and_state(): pl.pallas_call(conv_kernel, grid=(2, blocks), in_specs=in_specs, out_spec...  12.1 us
  transfers between devices with their start and end apart: 13, of which 9 were waited for; matrix products, arithmetic and copies ran while one was open for 6% of the time, Pallas kernels for 11%

profile of v3, /device:TPU:0, one launch (start us, length us, event | category | flops | bytes accessed | tf_op | source)
XLA Modules:
  0.0 229.8 jit_solution(2177375225998687143)
XLA Ops:
  2.6 1.1 slice_dynamic-update-slice_fusion.6
  3.7 1.1 slice_dynamic-update-slice_fusion.5
  5.9 1.4 copy.90
  7.4 5.4 %all-to-all-start = ((bf16[2,4,64,1832]{3,2,0,1:T(8,128)(2,1)}), bf16[2,4,64,1832]{3,2,0,1:T(8,128)(2,1)}, u32[]{:S(2)}, u32[]{:S(2)}) async-start(bf16[2,4,64,1832]{3,2,0,1:T(8,128)(2,1)} %copy.90), calls=%async_computation | async-start | bytes 3932160 | tf_op jit(solution)/shard_map/all_to_all | solution.py:344
  14.0 1.3 fusion.20
  15.4 21.6 %all-to-all-done = bf16[2,4,64,1832]{3,2,0,1:T(8,128)(2,1)} async-done(((bf16[2,4,64,1832]{3,2,0,1:T(8,128)(2,1)}), bf16[2,4,64,1832]{3,2,0,1:T(8,128)(2,1)}, u32[]{:S(2)}, u32[]{:S(2)}) %all-to-all-start) | async-done | bytes 1876000 | tf_op jit(solution)/shard_map/all_to_all | solution.py:344
  37.0 1.7 copy.91
  38.8 1.1 copy.110
  39.9 4.2 %all-to-all-start.4 = ((bf16[2,4,64,1024]{3,2,0,1:T(8,128)(2,1)}), bf16[2,4,64,1024]{3,2,0,1:T(8,128)(2,1)}, u32[]{:S(2)}, u32[]{:S(2)}) async-start(bf16[2,4,64,1024]{3,2,0,1:T(8,128)(2,1)} %copy.110), calls=%async_computation.4 | async-start | bytes 2097152 | tf_op jit(solution)/shard_map/all_to_all | solution.py:344
  44.1 2.8 %collective-permute-start = (bf16[2,3,1792]{2,1,0:T(4,128)(2,1)S(1)}, bf16[2,3,1792]{2,1,0:T(4,128)(2,1)S(1)}, u32[]{:S(2)}, u32[]{:S(2)}) collective-permute-start(bf16[2,3,1792]{2,1,0:T(4,128)(2,1)S(1)} %slice.226), channel_id=1, source_target_pairs={{0,16},{16,1},{1,17},{17,2},{2,18},{18,3},{3,19},{19,4},{4,20},{20... | collective-permute-start | bytes 64520 | tf_op jit(solution)/shard_map/ppermute | solution.py:381
  49.3 1.3 slice.241.refs_4_
  50.6 9.3 %collective-permute-done = bf16[2,3,1792]{2,1,0:T(4,128)(2,1)S(1)} collective-permute-done((bf16[2,3,1792]{2,1,0:T(4,128)(2,1)S(1)}, bf16[2,3,1792]{2,1,0:T(4,128)(2,1)S(1)}, u32[]{:S(2)}, u32[]{:S(2)}) %collective-permute-start) | collective-permute-done | bytes 21536 | tf_op jit(solution)/shard_map/ppermute | solution.py:381
  60.0 1.3 copy.111
  62.4 7.5 %conv_and_state.2 = (bf16[2,256,1536]{2,1,0:T(8,128)(2,1)S(1)}, bf16[2,4,400,128]{3,2,1,0:T(8,128)(2,1)}, bf16[2,256,256]{2,1,0:T(8,128)(2,1)S(1)}) custom-call(bf16[2,256,1832]{2,1,0:T(8,128)(2,1)S(1)} %bitcast.56, bf16[2,8,1792]{2,1,0:T(8,128)(2,1)S(1)} %pad.18.refs_1_.refs_7_, f32[4,1792]{1,0:T(4,128)S(1)} %get-tuple-element.33.refs_2_.refs_8_, ...), custom_call_target="tpu_custom_call" | custom-call | flops 6000000000 | bytes 5000000 | tf_op jit(solution)/shard_map/conv_and_state/pallas_call | solution.py:222
  69.8 1.1 copy-done.8
  71.1 4.7 %conv_and_state.3 = (bf16[2,256,1024]{2,1,0:T(8,128)(2,1)S(1)}, bf16[2,4,272,128]{3,2,1,0:T(8,128)(2,1)S(1)}) custom-call(bf16[2,256,1024]{2,1,0:T(8,128)(2,1)S(1)} %bitcast.61, bf16[2,8,1024]{2,1,0:T(8,128)(2,1)S(1)} %pad.20.refs_1_, f32[4,1024]{1,0:T(4,128)S(1)} %pad_maximum_fusion.4.refs_2_, f32[1,1024]{1,0:T(1,128)S(1)} %bitcast.64, ...), custom_call_target="tpu_custom_call" | custom-call | flops 6000000000 | bytes 5000000 | tf_op jit(solution)/shard_map/conv_and_state/pallas_call | solution.py:222
  75.8 19.5 %all_to_all.40.held_ref = bf16[8,272,128]{2,1,0:T(8,128)(2,1)S(1)} all-to-all(bf16[8,272,128]{2,1,0:T(8,128)(2,1)S(1)} %bitcast.63), channel_id=1, replica_groups={{0,1,2,3,16,17,18,19},{4,5,6,7,20,21,22,23},{8,9,10,11,24,25,26,27},{12..., dimensions={0} | all-to-all | bytes 1114112 | tf_op jit(solution)/shard_map/all_to_all | solution.py:416
  95.4 3.5 %all-to-all-start.1 = ((bf16[8,400,128]{2,1,0:T(8,128)(2,1)}), bf16[8,400,128]{2,1,0:T(8,128)(2,1)S(1)}, u32[]{:S(2)}, u32[]{:S(2)}) async-start(bf16[8,400,128]{2,1,0:T(8,128)(2,1)} %bitcast.17), calls=%async_computation.1 | async-start | bytes 1638400 | tf_op jit(solution)/shard_map/all_to_all | solution.py:416
  99.8 1.8 collective-permute-start.5
  101.6 2.6 %collective-permute-start.4 = (bf16[272,128]{1,0:T(8,128)(2,1)S(1)}, bf16[272,128]{1,0:T(8,128)(2,1)S(1)}, u32[]{:S(2)}, u32[]{:S(2)}) collective-permute-start(bf16[272,128]{1,0:T(8,128)(2,1)S(1)} %held_total.3), channel_id=1, source_target_pairs={{0,4},{4,8},{8,12},{12,16},{16,20},{20,24},{24,28},{1,5},{5,9},{9,... | collective-permute-start | bytes 208904 | tf_op jit(solution)/shard_map/ppermute | solution.py:449
  104.3 6.0 %collective-permute-done.5 = bf16[272,128]{1,0:T(8,128)(2,1)S(1)} collective-permute-done((bf16[272,128]{1,0:T(8,128)(2,1)S(1)}, bf16[272,128]{1,0:T(8,128)(2,1)S(1)}, u32[]{:S(2)}, u32[]{:S(2)}) %collective-permute-start.5) | collective-permute-done | bytes 69664 | tf_op jit(solution)/shard_map/ppermute | solution.py:449
  111.9 8.0 %all-to-all-done.1.held_ref = bf16[8,400,128]{2,1,0:T(8,128)(2,1)S(1)} async-done(((bf16[8,400,128]{2,1,0:T(8,128)(2,1)}), bf16[8,400,128]{2,1,0:T(8,128)(2,1)S(1)}, u32[]{:S(2)}, u32[]{:S(2)}) %all-to-all-start.1) | async-done | bytes 819232 | tf_op jit(solution)/shard_map/all_to_all | solution.py:416
  119.9 6.8 %all-to-all-start.6 = ((bf16[8,256,128]{2,1,0:T(8,128)(2,1)}), bf16[8,256,128]{2,1,0:T(8,128)(2,1)S(1)}, u32[]{:S(2)}, u32[]{:S(2)}) async-start(bf16[8,256,128]{2,1,0:T(8,128)(2,1)} %copy-done.7), calls=%async_computation.6 | async-start | bytes 1048576 | tf_op jit(solution)/shard_map/all_to_all | solution.py:416
  127.5 1.3 collective-permute-start.2
  128.8 2.3 collective-permute-start.1
  131.1 4.6 %collective-permute-done.2 = bf16[400,128]{1,0:T(8,128)(2,1)S(1)} collective-permute-done((bf16[400,128]{1,0:T(8,128)(2,1)S(1)}, bf16[400,128]{1,0:T(8,128)(2,1)S(1)}, u32[]{:S(2)}, u32[]{:S(2)}) %collective-permute-start.2) | collective-permute-done | bytes 102432 | tf_op jit(solution)/shard_map/ppermute | solution.py:449
  136.7 1.2 copy-done
  139.0 11.0 %all-to-all-start.2 = ((bf16[8,384,128]{2,1,0:T(8,128)(2,1)}), bf16[8,384,128]{2,1,0:T(8,128)(2,1)S(1)}, u32[]{:S(2)}, u32[]{:S(2)}) async-start(bf16[8,384,128]{2,1,0:T(8,128)(2,1)} %copy-done.6), calls=%async_computation.2 | async-start | bytes 1572864 | tf_op jit(solution)/shard_map/all_to_all | solution.py:416
  150.1 1.1 copy.106
  151.2 1.1 copy.103
  154.0 1.2 copy-done.11
  155.2 4.0 %mix.3.diag_ref = f32[2,256,1024]{2,1,0:T(8,128)S(1)} custom-call(bf16[2,256,1024]{2,1,0:T(8,128)(2,1)S(1)} %copy-done.11, bf16[2,256,256]{2,1,0:T(8,128)(2,1)S(1)} %copy-done.4, f32[2,4,256,4]{3,2,1,0:T(8,128)S(1)} %slice.243.col_ref, f32[2,4,4,256]{3,2,1,0:T(4,128)S(1)} %slice.244.row_ref, f32[1,1024]{1,0:T(1,128)S(1)} %pad_maximum_fusion.8.skip_ref), custom_call_target="tpu_custom_call" | custom-call | flops 4000000000 | bytes 4000000 | tf_op jit(solution)/shard_map/mix/pallas_call | solution.py:240
  159.2 2.3 add_carried.3
  162.6 6.0 %all-to-all-done.2 = bf16[8,384,128]{2,1,0:T(8,128)(2,1)S(1)} async-done(((bf16[8,384,128]{2,1,0:T(8,128)(2,1)}), bf16[8,384,128]{2,1,0:T(8,128)(2,1)S(1)}, u32[]{:S(2)}, u32[]{:S(2)}) %all-to-all-start.2) | async-done | bytes 786464 | tf_op jit(solution)/shard_map/all_to_all | solution.py:416
  168.5 4.3 %all-to-all-start.7 = ((bf16[2,4,64,1024]{3,2,0,1:T(8,128)(2,1)}), bf16[2,4,64,1024]{3,2,0,1:T(8,128)(2,1)}, u32[]{:S(2)}, u32[]{:S(2)}) async-start(bf16[2,4,64,1024]{3,2,0,1:T(8,128)(2,1)} %copy.112), calls=%async_computation.7 | async-start | bytes 2097152 | tf_op jit(solution)/shard_map/all_to_all | solution.py:344
  172.9 1.4 copy-done.9
  174.3 4.7 %mix.2.diag_ref = f32[2,256,1536]{2,1,0:T(8,128)S(1)} custom-call(bf16[2,256,1536]{2,1,0:T(8,128)(2,1)S(1)} %copy-done.9, bf16[2,256,256]{2,1,0:T(8,128)(2,1)S(1)} %copy-done.5, f32[2,4,256,6]{3,2,1,0:T(8,128)S(1)} %bitcast.46, f32[2,4,6,256]{3,2,1,0:T(8,128)S(1)} %slice.233.row_ref, f32[1,1536]{1,0:T(1,128)S(1)} %pad_maximum_fusion.6.skip_ref), custom_call_target="tpu_custom_call" | custom-call | flops 4000000000 | bytes 4000000 | tf_op jit(solution)/shard_map/mix/pallas_call | solution.py:240
  179.0 2.9 %add_carried.2 = bf16[2,256,1536]{2,1,0:T(8,128)(2,1)S(1)} custom-call(f32[2,256,1536]{2,1,0:T(8,128)S(1)} %mix.2.diag_ref, bf16[2,256,256]{2,1,0:T(8,128)(2,1)S(1)} %copy-done.5, f32[2,4,256,6]{3,2,1,0:T(8,128)S(1)} %bitcast.47, bf16[2,4,384,128]{3,2,1,0:T(8,128)(2,1)S(1)} %bitcast.52), custom_call_target="tpu_custom_call" | custom-call | tf_op jit(solution)/shard_map/add_carried/pallas_call | solution.py:264
  181.9 1.2 copy.108
  183.2 3.8 %all-to-all-done.7 = bf16[2,4,64,1024]{3,2,0,1:T(8,128)(2,1)} async-done(((bf16[2,4,64,1024]{3,2,0,1:T(8,128)(2,1)}), bf16[2,4,64,1024]{3,2,0,1:T(8,128)(2,1)}, u32[]{:S(2)}, u32[]{:S(2)}) %all-to-all-start.7) | async-done | bytes 1048608 | tf_op jit(solution)/shard_map/all_to_all | solution.py:344
  187.0 4.5 %all-to-all-start.3 = ((bf16[2,4,64,1536]{3,2,0,1:T(8,128)(2,1)}), bf16[2,4,64,1536]{3,2,0,1:T(8,128)(2,1)}, u32[]{:S(2)}, u32[]{:S(2)}) async-start(bf16[2,4,64,1536]{3,2,0,1:T(8,128)(2,1)} %copy.108), calls=%async_computation.3 | async-start | bytes 3145728 | tf_op jit(solution)/shard_map/all_to_all | solution.py:344
  191.5 1.7 pad_maximum_fusion
  193.2 1.3 copy.113
  194.6 16.5 %all-to-all-done.3 = bf16[2,4,64,1536]{3,2,0,1:T(8,128)(2,1)} async-done(((bf16[2,4,64,1536]{3,2,0,1:T(8,128)(2,1)}), bf16[2,4,64,1536]{3,2,0,1:T(8,128)(2,1)}, u32[]{:S(2)}, u32[]{:S(2)}) %all-to-all-start.3) | async-done | bytes 1572896 | tf_op jit(solution)/shard_map/all_to_all | solution.py:344
  211.0 1.5 copy.109
  213.0 1.3 copy-done.12
  214.3 1.8 multiply_reduce_fusion
  216.1 13.8 %convolution_convert_fusion = bf16[512,2560]{1,0:T(8,128)(2,1)} fusion(bf16[2560,2560]{1,0:T(8,128)(2,1)} %param.22, f32[2560]{0:T(1024)S(1)} %copy-done.21, f32[512]{0:T(512)S(1)} %add_rsqrt_fusion, bf16[512,2560]{1,0:T(8,128)(2,1)S(1)} %copy-done.12, bf16[512,2560]{1,0:T(8,128)(2,1)S(1)} %slice_dynamic-update-slice_fusion.8), kind=kOutput, calls=%fused_computation.9 | convolution fusion | flops 6725304320 | bytes 20983808 | tf_op jit(solution)/shard_map/dot_general | solution.py:468
  (127 shorter events, 16.7 us)
Async XLA Ops:
  0.6 5.2 %copy-start.15 = (bf16[512,256]{1,0:T(8,128)(2,1)S(1)}, bf16[512,256]{1,0:T(8,128)(2,1)}, u32[]{:S(2)}) copy-start(bf16[512,256]{1,0:T(8,128)(2,1)} %param.13) | copy-start | bytes 786436
  7.3 5.4 %copy-start.17 = (f32[2816]{0:T(1024)S(1)}, f32[2816]{0:T(1024)}, u32[]{:S(2)}) copy-start(f32[2816]{0:T(1024)} %param.17) | copy-start | bytes 33796
  7.4 5.4 %copy-start.18 = (s32[16]{0:T(128)S(1)}, s32[16]{0:T(128)}, u32[]{:S(2)}) copy-start(s32[16]{0:T(128)} %param.23) | copy-start | bytes 196
  7.4 6.5 %copy-start.16 = (f32[4,2816]{1,0:T(4,128)S(1)}, f32[4,2816]{1,0:T(4,128)}, u32[]{:S(2)}) copy-start(f32[4,2816]{1,0:T(4,128)} %param.16) | copy-start | bytes 135172
  7.4 29.7 %all-to-all-start = ((bf16[2,4,64,1832]{3,2,0,1:T(8,128)(2,1)}), bf16[2,4,64,1832]{3,2,0,1:T(8,128)(2,1)}, u32[]{:S(2)}, u32[]{:S(2)}) async-start(bf16[2,4,64,1832]{3,2,0,1:T(8,128)(2,1)} %copy.90), calls=%async_computation | async-start | bytes 3932160 | tf_op jit(solution)/shard_map/all_to_all | solution.py:344
  12.7 2.7 %copy-start.22 = (f32[40]{0:T(128)S(1)}, f32[40]{0:T(128)}, u32[]{:S(2)}) copy-start(f32[40]{0:T(128)} %param.19) | copy-start | bytes 484
  38.7 8.2 %copy-start.19 = (f32[40]{0:T(128)S(1)}, f32[40]{0:T(128)}, u32[]{:S(2)}) copy-start(f32[40]{0:T(128)} %param.18) | copy-start | bytes 484
  39.9 20.2 %all-to-all-start.4 = ((bf16[2,4,64,1024]{3,2,0,1:T(8,128)(2,1)}), bf16[2,4,64,1024]{3,2,0,1:T(8,128)(2,1)}, u32[]{:S(2)}, u32[]{:S(2)}) async-start(bf16[2,4,64,1024]{3,2,0,1:T(8,128)(2,1)} %copy.110), calls=%async_computation.4 | async-start | bytes 2097152 | tf_op jit(solution)/shard_map/all_to_all | solution.py:344
  44.1 15.8 %collective-permute-start = (bf16[2,3,1792]{2,1,0:T(4,128)(2,1)S(1)}, bf16[2,3,1792]{2,1,0:T(4,128)(2,1)S(1)}, u32[]{:S(2)}, u32[]{:S(2)}) collective-permute-start(bf16[2,3,1792]{2,1,0:T(4,128)(2,1)S(1)} %slice.226), channel_id=1, source_target_pairs={{0,16},{16,1},{1,17},{17,2},{2,18},{18,3},{3,19},{19,4},{4,20},{20... | collective-permute-start | bytes 64520 | tf_op jit(solution)/shard_map/ppermute | solution.py:381
  61.3 9.6 %collective-permute-start.3 = (bf16[2,3,1024]{2,1,0:T(4,128)(2,1)S(1)}, bf16[2,3,1024]{2,1,0:T(4,128)(2,1)S(1)}, u32[]{:S(2)}, u32[]{:S(2)}) collective-permute-start(bf16[2,3,1024]{2,1,0:T(4,128)(2,1)S(1)} %slice.239), channel_id=1, source_target_pairs={{0,16},{16,1},{1,17},{17,2},{2,18},{18,3},{3,19},{19,4},{4,20},{20... | collective-permute-start | bytes 36872 | tf_op jit(solution)/shard_map/ppermute | solution.py:381
  62.4 8.7 %copy-start.2 = (f32[2,4,256,4]{3,2,1,0:T(8,128)S(1)}, f32[2,4,256,4]{3,2,1,0:T(8,128)}, u32[]{:S(2)}) copy-start(f32[2,4,256,4]{3,2,1,0:T(8,128)} %slice.241.refs_4_) | copy-start | bytes 98308
  69.8 1.1 copy-start.8
  71.0 4.8 %copy-start.3 = (bf16[2,256,256]{2,1,0:T(8,128)(2,1)}, bf16[2,256,256]{2,1,0:T(8,128)(2,1)S(1)}, u32[]{:S(2)}) copy-start(bf16[2,256,256]{2,1,0:T(8,128)(2,1)S(1)} %get-tuple-element.13.bc_ref.refs_6_) | copy-start | bytes 786436
  75.8 19.6 %copy-start.10 = (bf16[2,256,1024]{2,1,0:T(8,128)(2,1)}, bf16[2,256,1024]{2,1,0:T(8,128)(2,1)S(1)}, u32[]{:S(2)}) copy-start(bf16[2,256,1024]{2,1,0:T(8,128)(2,1)S(1)} %get-tuple-element.17.x_ref) | copy-start | bytes 3145732
  95.4 24.6 %all-to-all-start.1 = ((bf16[8,400,128]{2,1,0:T(8,128)(2,1)}), bf16[8,400,128]{2,1,0:T(8,128)(2,1)S(1)}, u32[]{:S(2)}, u32[]{:S(2)}) async-start(bf16[8,400,128]{2,1,0:T(8,128)(2,1)} %bitcast.17), calls=%async_computation.1 | async-start | bytes 1638400 | tf_op jit(solution)/shard_map/all_to_all | solution.py:416
  99.8 10.5 %collective-permute-start.5 = (bf16[272,128]{1,0:T(8,128)(2,1)S(1)}, bf16[272,128]{1,0:T(8,128)(2,1)S(1)}, u32[]{:S(2)}, u32[]{:S(2)}) collective-permute-start(bf16[272,128]{1,0:T(8,128)(2,1)S(1)} %held_total.3), channel_id=1, source_target_pairs={{0,8},{4,12},{8,16},{12,20},{16,24},{20,28},{1,9},{5,13},{9,17},{1... | collective-permute-start | bytes 208904 | tf_op jit(solution)/shard_map/ppermute | solution.py:449
  101.6 8.7 %collective-permute-start.4 = (bf16[272,128]{1,0:T(8,128)(2,1)S(1)}, bf16[272,128]{1,0:T(8,128)(2,1)S(1)}, u32[]{:S(2)}, u32[]{:S(2)}) collective-permute-start(bf16[272,128]{1,0:T(8,128)(2,1)S(1)} %held_total.3), channel_id=1, source_target_pairs={{0,4},{4,8},{8,12},{12,16},{16,20},{20,24},{24,28},{1,5},{5,9},{9,... | collective-permute-start | bytes 208904 | tf_op jit(solution)/shard_map/ppermute | solution.py:449
  111.1 0.8 copy-start.7
  111.9 38.0 %copy-start.20 = (f32[40]{0:T(128)S(1)}, f32[40]{0:T(128)}, u32[]{:S(2)}) copy-start(f32[40]{0:T(128)} %param.20) | copy-start | bytes 484
  119.9 19.0 %all-to-all-start.6 = ((bf16[8,256,128]{2,1,0:T(8,128)(2,1)}), bf16[8,256,128]{2,1,0:T(8,128)(2,1)S(1)}, u32[]{:S(2)}, u32[]{:S(2)}) async-start(bf16[8,256,128]{2,1,0:T(8,128)(2,1)} %copy-done.7), calls=%async_computation.6 | async-start | bytes 1048576 | tf_op jit(solution)/shard_map/all_to_all | solution.py:416
  127.5 8.2 %collective-permute-start.2 = (bf16[400,128]{1,0:T(8,128)(2,1)S(1)}, bf16[400,128]{1,0:T(8,128)(2,1)S(1)}, u32[]{:S(2)}, u32[]{:S(2)}) collective-permute-start(bf16[400,128]{1,0:T(8,128)(2,1)S(1)} %held_total.2), channel_id=1, source_target_pairs={{0,8},{4,12},{8,16},{12,20},{16,24},{20,28},{1,9},{5,13},{9,17},{1... | collective-permute-start | bytes 307208 | tf_op jit(solution)/shard_map/ppermute | solution.py:449
  128.8 6.9 %collective-permute-start.1 = (bf16[400,128]{1,0:T(8,128)(2,1)S(1)}, bf16[400,128]{1,0:T(8,128)(2,1)S(1)}, u32[]{:S(2)}, u32[]{:S(2)}) collective-permute-start(bf16[400,128]{1,0:T(8,128)(2,1)S(1)} %held_total.2), channel_id=1, source_target_pairs={{0,4},{4,8},{8,12},{12,16},{16,20},{20,24},{24,28},{1,5},{5,9},{9,... | collective-permute-start | bytes 307208 | tf_op jit(solution)/shard_map/ppermute | solution.py:449
  136.7 1.2 copy-start
  137.9 0.9 copy-start.6
  139.0 29.6 %all-to-all-start.2 = ((bf16[8,384,128]{2,1,0:T(8,128)(2,1)}), bf16[8,384,128]{2,1,0:T(8,128)(2,1)S(1)}, u32[]{:S(2)}, u32[]{:S(2)}) async-start(bf16[8,384,128]{2,1,0:T(8,128)(2,1)} %copy-done.6), calls=%async_computation.2 | async-start | bytes 1572864 | tf_op jit(solution)/shard_map/all_to_all | solution.py:416
  151.2 1.1 copy-start.13
  153.1 1.0 copy-start.4
  154.0 1.2 copy-start.11
  161.5 11.3 %copy-start.14 = (f32[2,256,4,10]{1,3,2,0:T(8,128)S(1)}, f32[2,256,4,10]{1,3,2,0:T(8,128)}, u32[]{:S(2)}) copy-start(f32[2,256,4,10]{1,3,2,0:T(8,128)} %copy-done.13) | copy-start | bytes 245764
  161.5 11.3 %copy-start.5 = (bf16[2,256,256]{2,1,0:T(8,128)(2,1)S(1)}, bf16[2,256,256]{2,1,0:T(8,128)(2,1)}, u32[]{:S(2)}) copy-start(bf16[2,256,256]{2,1,0:T(8,128)(2,1)} %copy-done.3) | copy-start | bytes 786436
  168.5 18.5 %all-to-all-start.7 = ((bf16[2,4,64,1024]{3,2,0,1:T(8,128)(2,1)}), bf16[2,4,64,1024]{3,2,0,1:T(8,128)(2,1)}, u32[]{:S(2)}, u32[]{:S(2)}) async-start(bf16[2,4,64,1024]{3,2,0,1:T(8,128)(2,1)} %copy.112), calls=%async_computation.7 | async-start | bytes 2097152 | tf_op jit(solution)/shard_map/all_to_all | solution.py:344
  172.9 1.4 copy-start.9
  181.9 9.6 %copy-start.1 = (f32[8,384,128]{2,1,0:T(8,128)S(1)}, f32[8,384,128]{2,1,0:T(8,128)}, u32[]{:S(2)}) copy-start(f32[8,384,128]{2,1,0:T(8,128)} %copy-done) | copy-start | bytes 4718596
  187.0 24.0 %all-to-all-start.3 = ((bf16[2,4,64,1536]{3,2,0,1:T(8,128)(2,1)}), bf16[2,4,64,1536]{3,2,0,1:T(8,128)(2,1)}, u32[]{:S(2)}, u32[]{:S(2)}) async-start(bf16[2,4,64,1536]{3,2,0,1:T(8,128)(2,1)} %copy.108), calls=%async_computation.3 | async-start | bytes 3145728 | tf_op jit(solution)/shard_map/all_to_all | solution.py:344
  212.5 1.7 copy-start.12
  214.3 1.8 copy-start.21

commit v4 on v2

--- a/solution.py
+++ b/solution.py
@@ -12,7 +12,7 @@
 LMAX_CH = 16
 HIST = 8
 GAIN_ROWS = 16
-VMEM = 40 * 1024 * 1024
+VMEM = 60 * 1024 * 1024
 LOG2E = math.log2(math.e)
 
 

time: 211 us -> 225 us (1.066)
  Pallas kernels: 25.1 us -> 36.6 us
  waiting for transfers between devices: 93.3 us -> 88.8 us
  other arithmetic: 5.59 us -> 8.55 us
  matrix products: 8.96 us -> 11.8 us
    unnamed x41 -> x23, local copies, waits for them, and re-layouts: 13.1 us -> 4.61 us
    pallas_call x1, Pallas kernels: 4.31 us -> 8.47 us  [add_carried(): pl.pallas_call(carry_kernel, grid=(2, blocks), in_specs=[pl.BlockSpec((1,...]
    pallas_call x1, Pallas kernels: 6.24 us -> 9.58 us  [mix(): pl.pallas_call(mix_kernel, grid=(2, blocks), in_specs=[pl.BlockSpec((1, S...]
    dot_general x1, matrix products: 8.41 us -> 11.3 us  [per_device(): jnp.dot(normed, w_out, preferred_element_type=jnp.float32)]
    reshape x3, local copies, waits for them, and re-layouts: 1.71 us -> 4.23 us  [by_block(): return value.reshape(2, STRETCH, n_seq, heads_here)]
  transfers between devices with their start and end apart: 6 -> 6, of which waited for: 6 -> 4; matrix products, arithmetic and copies ran while one was open for 2% -> 6% of each run, Pallas kernels for 3% -> 4%
where the time goes in v4:
time: 225 us; the launch traced here: 224 us
  waiting for transfers between devices  88.8 us (39%)
  Pallas kernels  36.6 us (16%)
  blocking collectives  33.6 us (15%)
  starting transfers between devices  23 us (10%)
  local copies, waits for them, and re-layouts  21.2 us (9%)
  matrix products  11.8 us (5%)
  other arithmetic  8.55 us (4%)
    all_to_all x2, waiting for transfers between devices, by_heads(): lax.all_to_all(value, ('req', 'seq'), split_axis=0, concat_axis=0, tiled=...  51.9 us
    all_to_all x1, blocking collectives, gather_stretches(): lax.all_to_all(cut, 'req', split_axis=1, concat_axis=1, tiled=True, axis_...  33.6 us
    all_to_all x1, waiting for transfers between devices, gather_stretches(): lax.all_to_all(cut, 'req', split_axis=1, concat_axis=1, tiled=True, axis_...  33.6 us
    pallas_call x1, Pallas kernels, conv_and_state(): pl.pallas_call(conv_kernel, grid=(2, blocks), in_specs=[pl.BlockSpec((1,...  12.2 us
    dot_general x1, matrix products, per_device(): jnp.dot(normed, w_out, preferred_element_type=jnp.float32)  11.3 us
    all_to_all x2, starting transfers between devices, by_heads(): lax.all_to_all(value, ('req', 'seq'), split_axis=0, concat_axis=0, tiled=...  9.74 us
    pallas_call x1, Pallas kernels, mix(): pl.pallas_call(mix_kernel, grid=(2, blocks), in_specs=[pl.BlockSpec((1, S...  9.58 us
    pallas_call x1, Pallas kernels, add_carried(): pl.pallas_call(carry_kernel, grid=(2, blocks), in_specs=[pl.BlockSpec((1,...  8.47 us
  transfers between devices with their start and end apart: 6, of which 4 were waited for; matrix products, arithmetic and copies ran while one was open for 6% of the time, Pallas kernels for 4%

profile of v4, /device:TPU:0, one launch (start us, length us, event | category | flops | bytes accessed | tf_op | source)
XLA Modules:
  0.0 224.2 jit_solution(9953040631392815674)
XLA Ops:
  0.6 0.9 copy.79
  1.5 2.0 pad_maximum_fusion
  3.6 1.9 copy.80
  5.5 5.4 %all-to-all-start = ((bf16[2,4,64,2856]{3,2,0,1:T(8,128)(2,1)}), bf16[2,4,64,2856]{3,2,0,1:T(8,128)(2,1)}, u32[]{:S(2)}, u32[]{:S(2)}) async-start(bf16[2,4,64,2856]{3,2,0,1:T(8,128)(2,1)} %copy.80), calls=%async_computation | async-start | bytes 6029312 | tf_op jit(solution)/shard_map/all_to_all | solution.py:326
  10.9 0.1 reduce
  11.1 0.6 broadcast_in_dim.36.bias_ref.bc_bias_ref
  11.7 0.6 broadcast_add_fusion
  12.4 0.6 gather_fusion
  13.0 33.6 %all-to-all-done = bf16[2,4,64,2856]{3,2,0,1:T(8,128)(2,1)} async-done(((bf16[2,4,64,2856]{3,2,0,1:T(8,128)(2,1)}), bf16[2,4,64,2856]{3,2,0,1:T(8,128)(2,1)}, u32[]{:S(2)}, u32[]{:S(2)}) %all-to-all-start) | async-done | bytes 2924576 | tf_op jit(solution)/shard_map/all_to_all | solution.py:326
  46.6 2.1 copy.81
  48.7 0.7 slice.18
  49.4 2.7 %collective-permute-start = (bf16[2,3,2816]{2,1,0:T(4,128)(2,1)}, bf16[2,3,2816]{2,1,0:T(4,128)(2,1)}, u32[]{:S(2)}, u32[]{:S(2)}) collective-permute-start(bf16[2,3,2816]{2,1,0:T(4,128)(2,1)} %slice.18), channel_id=1, source_target_pairs={{0,16},{16,1},{1,17},{17,2},{2,18},{18,3},{3,19},{19,4},{4,20},{20... | collective-permute-start | bytes 101384 | tf_op jit(solution)/shard_map/ppermute | solution.py:343
  52.1 0.6 convolution_bitcast_fusion
  52.7 0.9 multiply_subtract_fusion
  53.7 0.6 fusion.20.gain_ref
  54.4 1.7 copy.86
  56.1 2.2 copy.87
  58.3 0.7 slice.19
  59.0 0.1 select_select_fusion
  59.2 0.7 pad.9.hist_ref.bc_hist_ref
  59.8 12.2 %conv_and_state.1 = (bf16[2,256,2560]{2,1,0:T(8,128)(2,1)}, bf16[2,256,256]{2,1,0:T(8,128)(2,1)}, bf16[2,4,656,128]{3,2,1,0:T(8,128)(2,1)}) custom-call(bf16[2,256,2856]{2,1,0:T(8,128)(2,1)} %bitcast.38, bf16[2,8,2816]{2,1,0:T(8,128)(2,1)} %pad.9.hist_ref.bc_hist_ref, f32[4,2816]{1,0:T(4,128)} %bc_weight_ref.1, ...), custom_call_target="tpu_custom_call" | custom-call | tf_op jit(solution)/shard_map/conv_and_state/pallas_call | solution.py:189
  72.1 3.8 %all-to-all-start.1 = ((bf16[8,656,128]{2,1,0:T(8,128)(2,1)}), bf16[8,656,128]{2,1,0:T(8,128)(2,1)S(1)}, u32[]{:S(2)}, u32[]{:S(2)}) async-start(bf16[8,656,128]{2,1,0:T(8,128)(2,1)} %bitcast.46), calls=%async_computation.1 | async-start | bytes 2686976 | tf_op jit(solution)/shard_map/all_to_all | solution.py:384
  75.9 0.6 dynamic-slice_convert_fusion.1.starts_ref
  76.5 32.3 %all-to-all-done.1.held_ref = bf16[8,656,128]{2,1,0:T(8,128)(2,1)S(1)} async-done(((bf16[8,656,128]{2,1,0:T(8,128)(2,1)}), bf16[8,656,128]{2,1,0:T(8,128)(2,1)S(1)}, u32[]{:S(2)}, u32[]{:S(2)}) %all-to-all-start.1) | async-done | bytes 1343520 | tf_op jit(solution)/shard_map/all_to_all | solution.py:384
  108.8 1.1 copy-done.1
  109.9 2.4 %held_total.1 = bf16[656,128]{1,0:T(8,128)(2,1)} custom-call(s32[8]{0:T(128)} %dynamic-slice_convert_fusion.1.starts_ref, bf16[8,656,128]{2,1,0:T(8,128)(2,1)} %copy-done.1), custom_call_target="tpu_custom_call" | custom-call | tf_op jit(solution)/shard_map/held_total/pallas_call | solution.py:263
  112.2 1.3 collective-permute-start.2
  113.5 3.9 %collective-permute-start.1 = (bf16[656,128]{1,0:T(8,128)(2,1)}, bf16[656,128]{1,0:T(8,128)(2,1)S(1)}, u32[]{:S(2)}, u32[]{:S(2)}) collective-permute-start(bf16[656,128]{1,0:T(8,128)(2,1)} %held_total.1), channel_id=1, source_target_pairs={{0,4},{4,8},{8,12},{12,16},{16,20},{20,24},{24,28},{1,5},{5,9},{9,... | collective-permute-start | bytes 503816 | tf_op jit(solution)/shard_map/ppermute | solution.py:397
  117.5 0.7 dynamic-slice_convert_fusion.finals_ref
  118.2 3.3 %collective-permute-done.1 = bf16[656,128]{1,0:T(8,128)(2,1)S(1)} collective-permute-done((bf16[656,128]{1,0:T(8,128)(2,1)}, bf16[656,128]{1,0:T(8,128)(2,1)S(1)}, u32[]{:S(2)}, u32[]{:S(2)}) %collective-permute-start.1) | collective-permute-done | bytes 167968 | tf_op jit(solution)/shard_map/ppermute | solution.py:397
  121.5 0.8 pad_maximum_fusion.1.arrived_ref
  122.2 3.9 %held_scan.1 = (bf16[8,640,128]{2,1,0:T(8,128)(2,1)}, f32[8,640,128]{2,1,0:T(8,128)}) custom-call(s32[8]{0:T(128)} %dynamic-slice_convert_fusion.1.starts_ref, s32[8]{0:T(128)} %dynamic-slice_convert_fusion.finals_ref, bf16[8,656,128]{2,1,0:T(8,128)(2,1)} %copy-done.1, bf16[2,656,128]{2,1,0:T(8,128)(2,1)} %pad_maximum_fusion.1.arrived_ref), custom_call_target="tpu_custom_call" | custom-call | tf_op jit(solution)/shard_map/held_scan/pallas_call | solution.py:278
  126.1 5.9 %all-to-all-start.2 = ((bf16[8,640,128]{2,1,0:T(8,128)(2,1)}), bf16[8,640,128]{2,1,0:T(8,128)(2,1)S(1)}, u32[]{:S(2)}, u32[]{:S(2)}) async-start(bf16[8,640,128]{2,1,0:T(8,128)(2,1)} %get-tuple-element.10), calls=%async_computation.2 | async-start | bytes 2621440 | tf_op jit(solution)/shard_map/all_to_all | solution.py:384
  132.2 0.7 broadcast_in_dim_reshape.3.skip_ref
  132.9 0.1 copy.93
  133.0 1.3 copy.94
  134.3 0.1 copy.96
  134.4 0.7 copy.103
  135.1 9.6 %mix.1.diag_ref = f32[2,256,2560]{2,1,0:T(8,128)} custom-call(bf16[2,256,2560]{2,1,0:T(8,128)(2,1)} %get-tuple-element.7.x_ref, bf16[2,256,256]{2,1,0:T(8,128)(2,1)} %get-tuple-element.8.bc_ref, f32[2,4,256,10]{3,2,1,0:T(8,128)} %bitcast.43, f32[2,4,10,256]{3,2,1,0:T(8,128)} %bitcast.52, f32[1,2560]{1,0:T(1,128)} %broadcast_in_dim_reshape.3.skip_ref), custom_call_target="tpu_custom_call" | custom-call | flops 15000000512 | bytes 8000000 | tf_op jit(solution)/shard_map/mix/pallas_call | solution.py:222
  144.7 19.6 %all-to-all-done.2 = bf16[8,640,128]{2,1,0:T(8,128)(2,1)S(1)} async-done(((bf16[8,640,128]{2,1,0:T(8,128)(2,1)}), bf16[8,640,128]{2,1,0:T(8,128)(2,1)S(1)}, u32[]{:S(2)}, u32[]{:S(2)}) %all-to-all-start.2) | async-done | bytes 1310752 | tf_op jit(solution)/shard_map/all_to_all | solution.py:384
  164.3 1.1 copy-done.2
  165.4 8.5 %add_carried.1 = bf16[2,256,2560]{2,1,0:T(8,128)(2,1)} custom-call(f32[2,256,2560]{2,1,0:T(8,128)} %mix.1.diag_ref, bf16[2,256,256]{2,1,0:T(8,128)(2,1)} %get-tuple-element.8.bc_ref, f32[2,4,256,10]{3,2,1,0:T(8,128)} %bitcast.44, bf16[2,4,640,128]{3,2,1,0:T(8,128)(2,1)} %bitcast.42), custom_call_target="tpu_custom_call" | custom-call | tf_op jit(solution)/shard_map/add_carried/pallas_call | solution.py:246
  173.9 1.9 copy.98
  175.8 33.6 %all_to_all.20 = bf16[2,4,64,2560]{3,2,0,1:T(8,128)(2,1)S(1)} all-to-all(bf16[2,4,64,2560]{3,2,0,1:T(8,128)(2,1)S(1)} %copy.98), channel_id=1, replica_groups={{0,4,8,12},{16,20,24,28},{1,5,9,13},{17,21,25,29},{2,6,10,14},{18,22,26..., dimensions={1} | all-to-all | bytes 5242880 | tf_op jit(solution)/shard_map/all_to_all | solution.py:326
  209.4 0.3 copy.99
  209.6 1.5 copy-done.3
  211.1 1.8 multiply_reduce_fusion
  212.9 11.3 %convolution_convert_fusion = bf16[512,2560]{1,0:T(8,128)(2,1)} fusion(bf16[2560,2560]{1,0:T(8,128)(2,1)} %param.22, f32[512,2560]{1,0:T(8,128)S(1)} %get-tuple-element.13, f32[2560]{0:T(1024)S(1)} %copy-done.9, f32[512]{0:T(512)S(1)} %add_rsqrt_fusion), kind=kOutput, calls=%fused_computation.9 | convolution fusion | flops 6716129280 | bytes 20983808 | tf_op jit(solution)/shard_map/dot_general | solution.py:409
  (35 shorter events, 0.6 us)
Async XLA Ops:
  5.5 5.4 %copy-start.5 = (s32[16]{0:T(128)S(1)}, s32[16]{0:T(128)}, u32[]{:S(2)}) copy-start(s32[16]{0:T(128)} %param.23) | copy-start | bytes 196
  5.5 5.6 %copy-start.4 = (f32[2816]{0:T(1024)S(1)}, f32[2816]{0:T(1024)}, u32[]{:S(2)}) copy-start(f32[2816]{0:T(1024)} %param.17) | copy-start | bytes 33796
  5.5 7.6 %copy-start.10 = (f32[40]{0:T(128)S(1)}, f32[40]{0:T(128)}, u32[]{:S(2)}) copy-start(f32[40]{0:T(128)} %param.19) | copy-start | bytes 484
  5.5 41.1 %all-to-all-start = ((bf16[2,4,64,2856]{3,2,0,1:T(8,128)(2,1)}), bf16[2,4,64,2856]{3,2,0,1:T(8,128)(2,1)}, u32[]{:S(2)}, u32[]{:S(2)}) async-start(bf16[2,4,64,2856]{3,2,0,1:T(8,128)(2,1)} %copy.80), calls=%async_computation | async-start | bytes 6029312 | tf_op jit(solution)/shard_map/all_to_all | solution.py:326
  13.0 39.1 %copy-start.6 = (f32[40]{0:T(128)S(1)}, f32[40]{0:T(128)}, u32[]{:S(2)}) copy-start(f32[40]{0:T(128)} %param.18) | copy-start | bytes 484
  48.6 11.2 %copy-start = (bf16[2,4,64,2856]{3,2,1,0:T(8,128)(2,1)}, bf16[2,4,64,2856]{3,2,1,0:T(8,128)(2,1)S(1)}, u32[]{:S(2)}) copy-start(bf16[2,4,64,2856]{3,2,1,0:T(8,128)(2,1)S(1)} %copy.81) | copy-start | bytes 8773636
  49.4 8.9 %collective-permute-start = (bf16[2,3,2816]{2,1,0:T(4,128)(2,1)}, bf16[2,3,2816]{2,1,0:T(4,128)(2,1)}, u32[]{:S(2)}, u32[]{:S(2)}) collective-permute-start(bf16[2,3,2816]{2,1,0:T(4,128)(2,1)} %slice.18), channel_id=1, source_target_pairs={{0,16},{16,1},{1,17},{17,2},{2,18},{18,3},{3,19},{19,4},{4,20},{20... | collective-permute-start | bytes 101384 | tf_op jit(solution)/shard_map/ppermute | solution.py:343
  72.1 45.3 %copy-start.7 = (s32[16]{0:T(128)S(1)}, s32[16]{0:T(128)}, u32[]{:S(2)}) copy-start(s32[16]{0:T(128)} %get-tuple-element.21) | copy-start | bytes 196
  72.1 36.7 %all-to-all-start.1 = ((bf16[8,656,128]{2,1,0:T(8,128)(2,1)}), bf16[8,656,128]{2,1,0:T(8,128)(2,1)S(1)}, u32[]{:S(2)}, u32[]{:S(2)}) async-start(bf16[8,656,128]{2,1,0:T(8,128)(2,1)} %bitcast.46), calls=%async_computation.1 | async-start | bytes 2686976 | tf_op jit(solution)/shard_map/all_to_all | solution.py:384
  76.5 55.6 %copy-start.8 = (f32[40]{0:T(128)S(1)}, f32[40]{0:T(128)}, u32[]{:S(2)}) copy-start(f32[40]{0:T(128)} %param.20) | copy-start | bytes 484
  108.8 1.1 copy-start.1
  112.2 5.9 %collective-permute-start.2 = (bf16[656,128]{1,0:T(8,128)(2,1)}, bf16[656,128]{1,0:T(8,128)(2,1)S(1)}, u32[]{:S(2)}, u32[]{:S(2)}) collective-permute-start(bf16[656,128]{1,0:T(8,128)(2,1)} %held_total.1), channel_id=1, source_target_pairs={{0,8},{4,12},{8,16},{12,20},{16,24},{20,28},{1,9},{5,13},{9,17},{1... | collective-permute-start | bytes 503816 | tf_op jit(solution)/shard_map/ppermute | solution.py:397
  113.5 7.9 %collective-permute-start.1 = (bf16[656,128]{1,0:T(8,128)(2,1)}, bf16[656,128]{1,0:T(8,128)(2,1)S(1)}, u32[]{:S(2)}, u32[]{:S(2)}) collective-permute-start(bf16[656,128]{1,0:T(8,128)(2,1)} %held_total.1), channel_id=1, source_target_pairs={{0,4},{4,8},{8,12},{12,16},{16,20},{20,24},{24,28},{1,5},{5,9},{9,... | collective-permute-start | bytes 503816 | tf_op jit(solution)/shard_map/ppermute | solution.py:397
  126.1 38.2 %all-to-all-start.2 = ((bf16[8,640,128]{2,1,0:T(8,128)(2,1)}), bf16[8,640,128]{2,1,0:T(8,128)(2,1)S(1)}, u32[]{:S(2)}, u32[]{:S(2)}) async-start(bf16[8,640,128]{2,1,0:T(8,128)(2,1)} %get-tuple-element.10), calls=%async_computation.2 | async-start | bytes 2621440 | tf_op jit(solution)/shard_map/all_to_all | solution.py:384
  164.3 1.1 copy-start.2
  209.4 1.7 copy-start.3
  211.1 1.8 copy-start.9
